TPU v7x, 32 devices: a whole 2x2x4 slice. The times are simulated.
32 devices in a mesh: cuts: 8 (over y, x, core), tile: 4 (over z).
Axes of the slice: x: 2, y: 2, z: 4, core: 2. Of those that a mesh axis runs over, the one named last changes fastest.
Arguments:
- probes: float32 [8, 8, 16, 4, 128], P('cuts', None, None, 'tile'), may hold values from -6 to 6
- test_block: float32 [8, 8, 16, 4, 128], P('cuts', None, None, 'tile'), may hold values from -6 to 6
- band_edge: float32 [8, 4, 128], P(None, 'tile'), may hold values from -3 to 3
- slice_hop: float32 [8], replicated, may hold values from 0.5 to 40
- cross_hop: float32 [2, 8, 8], replicated, may hold values from -0.4 to 0.4
- deform: float32 [6, 8, 8], replicated, may hold values from -0.4 to 0.4
- strain_elastic: float32 [8, 16, 6, 32], P('cuts', 'tile'), may hold values from -1 to 1
- strain_ids: int32 [16], replicated, may hold values from 0 to 15, as said below
Outputs:
- moment_fields: float32 [2, 2, 8, 8, 16, 4, 128], P(None, None, 'cuts', None, None, 'tile')
- projected: float32 [4, 2, 16, 16], replicated
Inputs may be any that keep to these rules, and one draw needn't show every extreme that they name: strain_ids is a permutation; subtile g belongs to index g // 4 of tile, and slots i belong to index i // 4. The 4 slots of one index of tile hold at most 2 subtiles belonging to any one index, and exactly 2 for some index.
All inputs are finite; a program needn't handle non-finite values.
Results may differ from a plain program's by a relative error of at most 0.0085.
Values sent between devices are 32-bit elements; how exact they have to be, the bound alone decides.
A program may use at most 128 MiB of HBM per device.

v0:
```python
import math

import jax
import jax.numpy as jnp
import numpy as np
from jax import lax
from jax.sharding import PartitionSpec as P

PTS = 8
NMOM = 4


HIGHEST = lax.Precision.HIGHEST


def extended(block, sides, width):
    for axis, dim in sides:
        count = lax.axis_size(axis)
        forward = [(i, i + 1) for i in range(count - 1)]
        backward = [(target, source) for source, target in forward]
        low = lax.ppermute(
            lax.slice_in_dim(block, block.shape[dim] - width, None, axis=dim), axis, forward
        )
        high = lax.ppermute(lax.slice_in_dim(block, 0, width, axis=dim), axis, backward)
        block = jnp.concatenate([low, block, high], axis=dim)
    return block


def complex_times(former, latter):
    return jnp.stack(
        [
            former[0] * latter[0] - former[1] * latter[1],
            former[0] * latter[1] + former[1] * latter[0],
        ]
    )


def complex_inverse(number):
    square = number[0] * number[0] + number[1] * number[1]
    return jnp.stack([number[0] / square, -number[1] / square])


def complex_power(base_value, exponent, bit_count):
    result = jnp.stack([jnp.ones_like(base_value[0]), jnp.zeros_like(base_value[0])])
    squared = base_value
    for bit_index in range(bit_count):
        bit_set = exponent // 2**bit_index % 2
        result = jnp.where(bit_set == 1, complex_times(result, squared), result)
        squared = complex_times(squared, squared)
    return result


def line_ratio(band_edge, slice_hop, real_part, imag_part):
    hopping = slice_hop[:, None, None]
    ratio_re = (real_part - band_edge) / hopping
    ratio_im = (imag_part + 0.0 * band_edge) / hopping
    disc_re = ratio_re * ratio_re - ratio_im * ratio_im - 4.0
    disc_im = 2.0 * ratio_re * ratio_im
    modulus = jnp.sqrt(disc_re * disc_re + disc_im * disc_im)
    root_re = jnp.sqrt(jnp.maximum(0.5 * (modulus + disc_re), 0.0))
    root_im = jnp.sqrt(jnp.maximum(0.5 * (modulus - disc_re), 0.0)) * jnp.where(
        disc_im >= 0.0, 1.0, -1.0
    )
    lower_re = 0.5 * (ratio_re - root_re)
    lower_im = 0.5 * (ratio_im - root_im)
    upper_re = 0.5 * (ratio_re + root_re)
    upper_im = 0.5 * (ratio_im + root_im)
    choose_low = (
        lower_re * lower_re + lower_im * lower_im <= upper_re * upper_re + upper_im * upper_im
    )
    alpha_re = jnp.where(choose_low, lower_re, upper_re)
    alpha_im = jnp.where(choose_low, lower_im, upper_im)
    return jnp.stack([-alpha_re, -alpha_im])


def line_kernel(decay_rate, slice_hop, length):
    bit_count = length.bit_length()
    exponents = jnp.arange(length + 1).reshape(-1, 1, 1, 1)
    powers = complex_power(decay_rate[:, None], exponents, bit_count)
    series = powers[:, :length] + powers[:, length:0:-1]
    unit_value = jnp.stack([jnp.ones_like(decay_rate[0]), jnp.zeros_like(decay_rate[0])])
    denominator = complex_times(
        unit_value - complex_times(decay_rate, decay_rate), unit_value - powers[:, length]
    )
    leading = complex_times(
        -decay_rate / slice_hop[None, :, None, None], complex_inverse(denominator)
    )
    profile = complex_times(leading[:, None], series)
    offsets = (np.arange(length)[:, None] - np.arange(length)[None, :]) % length
    return jnp.take(profile, jnp.asarray(offsets, dtype=jnp.int32), axis=1)


def relayout_strain(strain_elastic, strain_ids, rows, cols):
    tile_count = lax.axis_size("tile")
    my_tile = lax.axis_index("tile")
    slot_data = strain_elastic[0]
    sub_count = slot_data.shape[0]
    capacity = sub_count // 2
    id_table = strain_ids.reshape(tile_count, sub_count)
    destination = id_table // sub_count
    row_within = id_table % sub_count
    earlier = jnp.arange(sub_count)[:, None] < jnp.arange(sub_count)[None, :]
    matches = destination[:, :, None] == destination[:, None, :]
    rank_table = jnp.sum((matches & earlier[None]).astype(jnp.int32), axis=1)
    my_dest = lax.dynamic_index_in_dim(destination, my_tile, 0, False)
    my_rank = lax.dynamic_index_in_dim(rank_table, my_tile, 0, False)
    slot_index = my_dest * capacity + my_rank
    selector = (jnp.arange(tile_count * capacity)[:, None] == slot_index[None, :]).astype(
        jnp.float32
    )
    outgoing = jnp.dot(selector, slot_data.reshape(sub_count, -1), precision=HIGHEST)
    outgoing = outgoing.reshape(tile_count, capacity, -1)
    incoming = lax.all_to_all(outgoing, "tile", split_axis=0, concat_axis=0, tiled=True)
    hits = (destination == my_tile).astype(jnp.float32)
    row_onehot = (row_within[None, :, :] == jnp.arange(sub_count)[:, None, None]).astype(
        jnp.float32
    )
    rank_onehot = (rank_table[:, :, None] == jnp.arange(capacity)[None, None, :]).astype(
        jnp.float32
    )
    mapping = jnp.einsum("rps,ps,psk->rpk", row_onehot, hits, rank_onehot, precision=HIGHEST)
    gathered = jnp.dot(
        mapping.reshape(sub_count, tile_count * capacity),
        incoming.reshape(tile_count * capacity, -1),
        precision=HIGHEST,
    )
    return jnp.transpose(gathered.reshape(sub_count, 6, -1), (1, 0, 2)).reshape(6, rows, cols)


def couple_cells(amplitude, cross_hop, strain_mix):
    padded_rows = extended(amplitude, (("tile", 4),), 1)
    upward = padded_rows[:, :, :, :, 2:]
    downward = padded_rows[:, :, :, :, :-2]
    widths = [(0, 0)] * 5
    toward_right = jnp.pad(amplitude[..., 1:], widths + [(0, 1)])
    toward_left = jnp.pad(amplitude[..., :-1], widths + [(1, 0)])
    hoppers = jnp.stack([cross_hop[0], cross_hop[0].T, cross_hop[1], cross_hop[1].T])
    nearby = jnp.stack([toward_right, toward_left, upward, downward])
    summed = jnp.einsum("dbc,dktcpyx->ktbpyx", hoppers, nearby, precision=HIGHEST)
    return summed + jnp.einsum("bcyx,ktcpyx->ktbpyx", strain_mix, amplitude, precision=HIGHEST)


def gathered_kernel(decay_rate, slice_hop, cut_count, my_cut):
    narrow = decay_rate.shape[-1] // cut_count
    kernels = []
    for point in range(decay_rate.shape[1]):
        columns = lax.dynamic_slice_in_dim(decay_rate[:, point], my_cut * narrow, narrow, 3)
        kernels.append(line_kernel(columns, slice_hop, cut_count))
    return jnp.stack(kernels, axis=1)


def gathered_solver(kernel):

    def lines(received):

        def contract(former, latter):
            return jnp.einsum("tsmbyx,tbpmyx->tbpsyx", former, latter, precision=HIGHEST)

        return jnp.stack(
            [
                contract(kernel[0], received[0]) - contract(kernel[1], received[1]),
                contract(kernel[0], received[1]) + contract(kernel[1], received[0]),
            ]
        )

    def solve(residual):
        spread = lines(
            lax.all_to_all(
                residual[:, :, :, :, None], "cuts", split_axis=6, concat_axis=4, tiled=True
            )
        )
        back_home = lax.all_to_all(spread, "cuts", split_axis=4, concat_axis=6, tiled=True)
        return back_home[:, :, :, :, 0]

    return solve


def on_device(
    probes, test_block, band_edge, slice_hop, cross_hop, deform, strain_elastic, strain_ids
):
    amplitude = probes[0]
    testing = test_block[0]
    bands, probe_count, rows, cols = amplitude.shape
    cut_count = lax.axis_size("cuts")
    my_cut = lax.axis_index("cuts")
    tile_count = lax.axis_size("tile")
    strain_cells = relayout_strain(strain_elastic, strain_ids, rows, cols)
    symmetric = 0.5 * (deform + jnp.transpose(deform, (0, 2, 1)))
    strain_mix = jnp.einsum("kyx,kbc->bcyx", strain_cells, symmetric, precision=HIGHEST)
    scale = (cut_count * bands * rows * tile_count * cols) ** (-0.5)
    angles = [math.pi * (2 * point + 1) / PTS for point in range(PTS)]
    decay_rate = jnp.stack(
        [line_ratio(band_edge, slice_hop, math.cos(angle), math.sin(angle)) for angle in angles],
        axis=1,
    )
    solver = gathered_solver(gathered_kernel(decay_rate, slice_hop, cut_count, my_cut))
    source = jnp.stack([amplitude, jnp.zeros_like(amplitude)])
    source = jnp.broadcast_to(source[:, None], (2, PTS) + amplitude.shape)
    first_step = solver(source)
    second_step = first_step + solver(couple_cells(first_step, cross_hop, strain_mix))
    tested = jnp.einsum("bqyx,ktbryx->ktqr", testing, second_step, precision=HIGHEST)
    weight_re = jnp.asarray(
        np.array(
            [[math.cos((order + 1) * angle) / PTS for angle in angles] for order in range(NMOM)],
            dtype=np.float32,
        )
    )
    weight_im = jnp.asarray(
        np.array(
            [[math.sin((order + 1) * angle) / PTS for angle in angles] for order in range(NMOM)],
            dtype=np.float32,
        )
    )
    projected = jnp.stack(
        [
            jnp.einsum("nt,tqr->nqr", weight_re, tested[0], precision=HIGHEST)
            - jnp.einsum("nt,tqr->nqr", weight_im, tested[1], precision=HIGHEST),
            jnp.einsum("nt,tqr->nqr", weight_re, tested[1], precision=HIGHEST)
            + jnp.einsum("nt,tqr->nqr", weight_im, tested[0], precision=HIGHEST),
        ],
        axis=1,
    )
    fields = jnp.stack(
        [
            jnp.einsum("nt,tbpyx->nbpyx", weight_re[:2], second_step[0], precision=HIGHEST)
            - jnp.einsum("nt,tbpyx->nbpyx", weight_im[:2], second_step[1], precision=HIGHEST),
            jnp.einsum("nt,tbpyx->nbpyx", weight_re[:2], second_step[1], precision=HIGHEST)
            + jnp.einsum("nt,tbpyx->nbpyx", weight_im[:2], second_step[0], precision=HIGHEST),
        ],
        axis=1,
    )
    projected = lax.psum(projected * scale, ("cuts", "tile"))
    return (fields[:, :, None], projected)


def solution(mesh):
    placed = (
        P("cuts", None, None, "tile", None),
        P("cuts", None, None, "tile", None),
        P(None, "tile", None),
        P(),
        P(),
        P(),
        P("cuts", "tile", None, None),
        P(),
    )
    return jax.shard_map(
        on_device,
        mesh=mesh,
        in_specs=placed,
        out_specs=(P(None, None, "cuts", None, None, "tile", None), P()),
        check_vma=False,
    )
```

profile of v0, /device:TPU:0, one launch (start us, length us, event | category | flops | bytes accessed | tf_op | source)
XLA Modules:
  0.0 452.8 jit_solution(363793928169127103)
XLA Ops:
  6.1 8.2 %reshape.3184 = f32[8,1,32768]{2,1,0:T(1,128)} reshape(f32[128,2,1,1,8,8,16]{6,5,4,3,2,1,0:T(8,128)} %broadcast_bitcast_fusion) | data formatting | bytes 2097152
  69.3 6.1 %reshape.3185 = f32[128,2,1,1,8,8,16]{6,5,4,3,2,1,0:T(8,128)} reshape(f32[8,32768]{1,0:T(8,128)S(1)} %reduce) | data formatting | bytes 2097152
  79.8 11.8 %fusion.15 = f32[8,8,16,16,8]{3,4,2,1,0:T(8,128)S(1)} fusion(f32[8,8,16,8,16]{2,1,0,4,3:T(8,128)S(1)} %bitcast.613, f32[2,8,8,8,8,1,16]{3,2,6,4,1,5,0:T(8,128)} %bitcast_dynamic-update-slice_fusion), kind=kOutput, calls=%fused_computation.32 | convolution fusion | flops 12582912 | bytes 5242880 | tf_op jit(solution)/shard_map/tsmbyx,tbpmyx->tbpsyx/dot_general | solution.py:157
  91.6 12.5 %fusion.17 = f32[8,8,16,16,8]{3,4,2,1,0:T(8,128)S(1)} fusion(f32[8,8,16,8,16]{2,1,0,4,3:T(8,128)S(1)} %bitcast.614, f32[2,8,8,8,8,1,16]{3,2,6,4,1,5,0:T(8,128)} %bitcast_dynamic-update-slice_fusion), kind=kOutput, calls=%fused_computation.34 | convolution fusion | flops 12582912 | bytes 5242880 | tf_op jit(solution)/shard_map/tsmbyx,tbpmyx->tbpsyx/dot_general | solution.py:157
  104.1 10.2 %subtract_bitcast_fusion.1 = f32[1,8,8,16,8,1,16]{3,4,6,2,1,5,0:T(8,128)S(1)} fusion(f32[8,8,16,16,8]{3,4,2,1,0:T(8,128)S(1)} %fusion.17, f32[2,8,8,8,8,1,16]{3,2,6,4,1,5,0:T(8,128)S(1)} %bitcast.607, f32[8,8,16,8,16]{2,1,0,4,3:T(8,128)S(1)} %bitcast.619), kind=kOutput, calls=%fused_computation.23 | convolution fusion | flops 12713984 | bytes 13107200 | tf_op jit(solution)/shard_map/tsmbyx,tbpmyx->tbpsyx/dot_general | solution.py:157
  114.4 10.4 %add_bitcast_fusion.1 = f32[1,8,8,16,8,1,16]{3,4,6,2,1,5,0:T(8,128)S(1)} fusion(f32[8,8,16,16,8]{3,4,2,1,0:T(8,128)S(1)} %fusion.15, f32[2,8,8,8,8,1,16]{3,2,6,4,1,5,0:T(8,128)S(1)} %bitcast.607, f32[8,8,16,8,16]{2,1,0,4,3:T(8,128)S(1)} %bitcast.620), kind=kOutput, calls=%fused_computation.22 | convolution fusion | flops 12713984 | bytes 13107200 | tf_op jit(solution)/shard_map/tsmbyx,tbpmyx->tbpsyx/dot_general | solution.py:157
  131.3 8.1 %reshape.3186 = f32[8,1,32768]{2,1,0:T(1,128)} reshape(f32[8,2,1,8,8,16,16]{6,5,4,3,2,1,0:T(8,128)} %bitcast.625) | data formatting | bytes 2097152
  145.9 13.5 %all-to-all-done.1 = f32[8,1,32768]{2,1,0:T(1,128)S(1)} async-done(((f32[8,1,32768]{2,1,0:T(1,128)}), f32[8,1,32768]{2,1,0:T(1,128)S(1)}, u32[]{:S(2)}, u32[]{:S(2)}) %all-to-all-start.1) | async-done | bytes 1048608 | tf_op jit(solution)/shard_map/all_to_all | solution.py:172
  162.6 6.1 %reshape.3187 = f32[8,2,1,8,8,16,16]{6,5,4,3,2,1,0:T(8,128)} reshape(f32[8,32768]{1,0:T(8,128)S(1)} %reduce.1) | data formatting | bytes 2097152
  168.7 9.2 %copy.335 = f32[2,8,8,16,8,1,16]{3,2,1,0,6,4,5:T(8,128)} copy(f32[2,8,8,16,8,1,16]{3,6,2,1,5,0,4:T(8,128)} %bitcast.610) | data formatting | bytes 2097152 | tf_op jit(solution)/shard_map/reshape.256
  177.9 8.7 %copy.284 = f32[2,8,8,16,8,1,16]{6,4,3,2,1,0,5:T(8,128)} copy(f32[2,8,8,16,8,1,16]{3,6,2,1,5,0,4:T(8,128)} %bitcast.611) | data formatting | bytes 2097152 | tf_op jit(solution)/shard_map/all_to_all | solution.py:172
  186.6 5.6 %squeeze.15 = f32[2,8,8,16,1,128]{5,3,2,1,0,4:T(8,128)S(1)} reshape(f32[2,8,8,16,8,1,16]{6,4,3,2,1,0,5:T(8,128)} %copy.284) | data formatting | bytes 2097152 | tf_op jit(solution)/shard_map/squeeze | solution.py:173
  193.9 5.5 %collective-permute-start.1 = (f32[2,8,8,16,1,128]{5,2,3,1,0,4:T(8,128)S(1)}, f32[2,8,8,16,1,128]{5,2,3,1,0,4:T(8,128)}, u32[]{:S(2)}, u32[]{:S(2)}) collective-permute-start(f32[2,8,8,16,1,128]{5,2,3,1,0,4:T(8,128)S(1)} %copy.285), channel_id=1, source_target_pairs={{0,1},{1,2},{2,3},{4,5},{5,6},{6,7},{8,9},{9,10},{10,11},{12,13},{... | collective-permute-start | bytes 3145736 | tf_op jit(solution)/shard_map/ppermute | solution.py:21
  199.4 11.6 %fusion.98 = f32[128,2,8,16,8]{3,4,2,1,0:T(8,128)} fusion(f32[2,8,8,16,128]{3,2,1,0,4:T(8,128)} %bitcast.622, f32[8,8,128,1,1]{1,0,4,3,2:T(8,128)S(1)} %copy-done.1), kind=kOutput, calls=%fused_computation.560 | convolution fusion | flops 25165824 | bytes 2129920 | tf_op jit(solution)/shard_map/bcyx,ktcpyx->ktbpyx/dot_general | solution.py:140
  211.1 7.5 %copy.300 = f32[128,2,8,16,8]{0,4,3,2,1:T(8,128)} copy(f32[128,2,8,16,8]{3,4,2,1,0:T(8,128)} %fusion.98) | data formatting | bytes 2097152 | tf_op jit(solution)/shard_map/bcyx,ktcpyx->ktbpyx/dot_general | solution.py:140
  223.6 7.5 %copy.301 = f32[2,8,8,16,1,1,128]{3,2,5,4,1,0,6:T(8,128)} copy(f32[2,8,8,16,1,1,128]{6,2,3,1,0,5,4:T(8,128)S(1)} %fusion.33) | data formatting | bytes 2097152 | tf_op jit(solution)/shard_map/broadcast_in_dim | solution.py:169
  231.1 7.1 %reshape.3188 = f32[8,1,32768]{2,1,0:T(1,128)S(1)} reshape(f32[128,2,8,1,1,8,16]{6,5,4,3,2,1,0:T(8,128)} %bitcast.621) | data formatting | bytes 2097152
  238.2 18.9 %all_to_all.20 = f32[8,1,32768]{2,1,0:T(1,128)} all-to-all(f32[8,1,32768]{2,1,0:T(1,128)S(1)} %reshape.3188), channel_id=1, replica_groups=mesh['cuts'=8,'tile'=4] {'cuts'}, dimensions={0} | all-to-all | bytes 2097152 | tf_op jit(solution)/shard_map/all_to_all | solution.py:168
  261.5 6.1 %reshape.3189 = f32[128,2,8,1,1,8,16]{6,5,4,3,2,1,0:T(8,128)} reshape(f32[8,32768]{1,0:T(8,128)S(1)} %reduce.2) | data formatting | bytes 2097152
  272.0 11.8 %fusion.7 = f32[8,8,16,16,8]{3,4,2,1,0:T(8,128)S(1)} fusion(f32[8,8,16,8,16]{2,1,0,4,3:T(8,128)S(1)} %bitcast.615, f32[2,8,8,8,8,1,16]{3,2,6,4,1,5,0:T(8,128)} %bitcast_dynamic-update-slice_fusion), kind=kOutput, calls=%fused_computation.24 | convolution fusion | flops 12582912 | bytes 5242880 | tf_op jit(solution)/shard_map/tsmbyx,tbpmyx->tbpsyx/dot_general | solution.py:157
  283.8 12.5 %fusion.9 = f32[8,8,16,16,8]{3,4,2,1,0:T(8,128)S(1)} fusion(f32[8,8,16,8,16]{2,1,0,4,3:T(8,128)S(1)} %bitcast.616, f32[2,8,8,8,8,1,16]{3,2,6,4,1,5,0:T(8,128)} %bitcast_dynamic-update-slice_fusion), kind=kOutput, calls=%fused_computation.26 | convolution fusion | flops 12582912 | bytes 5242880 | tf_op jit(solution)/shard_map/tsmbyx,tbpmyx->tbpsyx/dot_general | solution.py:157
  296.3 10.2 %subtract_bitcast_fusion = f32[1,8,8,16,8,1,16]{3,4,6,2,1,5,0:T(8,128)S(1)} fusion(f32[8,8,16,16,8]{3,4,2,1,0:T(8,128)S(1)} %fusion.9, f32[2,8,8,8,8,1,16]{3,2,6,4,1,5,0:T(8,128)S(1)} %bitcast.609, f32[8,8,16,8,16]{2,1,0,4,3:T(8,128)S(1)} %bitcast.617), kind=kOutput, calls=%fused_computation.21 | convolution fusion | flops 12713984 | bytes 13107200 | tf_op jit(solution)/shard_map/tsmbyx,tbpmyx->tbpsyx/dot_general | solution.py:157
  306.5 10.4 %add_bitcast_fusion = f32[1,8,8,16,8,1,16]{3,4,6,2,1,5,0:T(8,128)S(1)} fusion(f32[8,8,16,16,8]{3,4,2,1,0:T(8,128)S(1)} %fusion.7, f32[2,8,8,8,8,1,16]{3,2,6,4,1,5,0:T(8,128)S(1)} %bitcast.609, f32[8,8,16,8,16]{2,1,0,4,3:T(8,128)S(1)} %bitcast.618), kind=kOutput, calls=%fused_computation.20 | convolution fusion | flops 12713984 | bytes 13107200 | tf_op jit(solution)/shard_map/tsmbyx,tbpmyx->tbpsyx/dot_general | solution.py:157
  323.4 7.1 %reshape.3190 = f32[8,1,32768]{2,1,0:T(1,128)S(1)} reshape(f32[8,2,1,8,8,16,16]{6,5,4,3,2,1,0:T(8,128)} %bitcast.626) | data formatting | bytes 2097152
  330.6 18.9 %all_to_all.42 = f32[8,1,32768]{2,1,0:T(1,128)} all-to-all(f32[8,1,32768]{2,1,0:T(1,128)S(1)} %reshape.3190), channel_id=1, replica_groups=mesh['cuts'=8,'tile'=4] {'cuts'}, dimensions={0} | all-to-all | bytes 2097152 | tf_op jit(solution)/shard_map/all_to_all | solution.py:172
  353.8 6.1 %reshape.3191 = f32[8,2,1,8,8,16,16]{6,5,4,3,2,1,0:T(8,128)} reshape(f32[8,32768]{1,0:T(8,128)S(1)} %reduce.3) | data formatting | bytes 2097152
  359.9 11.8 %bitcast_add_fusion.1 = f32[2,8,8,16,8,1,16]{3,6,2,1,5,0,4:T(8,128)} fusion(f32[8,2,1,8,8,16,16]{6,5,4,3,2,1,0:T(8,128)} %reshape.3191, f32[8,2,1,8,8,16,16]{6,5,4,3,2,1,0:T(8,128)} %reshape.3187), kind=kLoop, calls=%fused_computation.559 | loop fusion | flops 262144 | bytes 3145728 | tf_op jit(solution)/shard_map/add | solution.py:200
  371.8 10.9 %copy.345 = f32[2,8,8,16,8,1,16]{6,4,1,3,2,0,5:T(8,128)} copy(f32[2,8,8,16,8,1,16]{3,6,2,1,5,0,4:T(8,128)} %bitcast.612) | data formatting | bytes 2097152 | tf_op jit(solution)/shard_map/squeeze | solution.py:173
  382.6 6.5 %reshape.3183 = f32[2,8,8,16,1,128]{5,1,3,2,4,0:T(8,128)} reshape(f32[2,8,8,16,8,1,16]{6,4,1,3,2,0,5:T(8,128)} %copy.345) | data formatting | bytes 2097152 | tf_op jit(solution)/shard_map/squeeze | solution.py:173
  392.1 8.7 %copy.312 = f32[2,8,8,16,8,1,16]{6,4,3,2,1,0,5:T(8,128)} copy(f32[2,8,8,16,8,1,16]{3,6,2,1,5,0,4:T(8,128)} %bitcast_add_fusion.1) | data formatting | bytes 2097152 | tf_op jit(solution)/shard_map/add | solution.py:200
  400.8 5.7 %add.1124 = f32[2,8,8,16,128]{4,3,2,1,0:T(8,128)S(1)} reshape(f32[2,8,8,16,8,1,16]{6,4,3,2,1,0,5:T(8,128)} %copy.312) | data formatting | bytes 2097152 | tf_op jit(solution)/shard_map/add | solution.py:200
  408.6 41.1 %psum.7 = f32[4,2,16,16]{3,0,2,1:T(4,128)S(1)} all-reduce(f32[4,2,16,16]{3,0,2,1:T(4,128)S(1)} %maximum_multiply_fusion), channel_id=1, replica_groups=mesh['cuts'=8,'tile'=4] {'cuts','tile'}, use_global_device_ids=true, to_apply=%region_1.3 | all-reduce | flops 2048 | bytes 16384 | tf_op jit(solution)/shard_map/psum | solution.py:232
  (240 shorter events, 114.0 us)
Async XLA Ops:
  0.6 406.0 %copy-start = (f32[1,8,16,1,128]{4,3,2,1,0:T(1,128)S(1)}, f32[1,8,16,1,128]{4,3,2,1,0:T(1,128)}, u32[]{:S(2)}) copy-start(f32[1,8,16,1,128]{4,3,2,1,0:T(1,128)} %param.21) | copy-start | bytes 196612
  6.0 13.5 %copy-start.15 = (s32[16]{0:T(128)S(1)}, s32[16]{0:T(128)}, u32[]{:S(2)}) copy-start(s32[16]{0:T(128)} %param.27) | copy-start | bytes 196
  6.0 13.6 %copy-start.16 = (s32[64]{0:T(128)S(1)}, s32[64]{0:T(128)}, u32[]{:S(2)}) copy-start(s32[64]{0:T(128)} %constant.541) | copy-start | bytes 772
  6.0 13.6 %copy-start.5 = (f32[1,4,6,32]{3,1,2,0:T(4,128)S(1)}, f32[1,4,6,32]{3,1,2,0:T(4,128)}, u32[]{:S(2)}) copy-start(f32[1,4,6,32]{3,1,2,0:T(4,128)} %param.26) | copy-start | bytes 9220
  6.0 13.7 %copy-start.7 = (f32[2,8,8]{2,1,0:T(8,128)S(1)}, f32[2,8,8]{2,1,0:T(8,128)}, u32[]{:S(2)}) copy-start(f32[2,8,8]{2,1,0:T(8,128)} %param.24) | copy-start | bytes 1540
  6.0 13.8 %copy-start.3 = (f32[6,8,8]{2,1,0:T(8,128)S(1)}, f32[6,8,8]{2,1,0:T(8,128)}, u32[]{:S(2)}) copy-start(f32[6,8,8]{2,1,0:T(8,128)} %param.25) | copy-start | bytes 4612
  6.0 13.9 %copy-start.13 = (f32[8,1,128]{2,1,0:T(1,128)S(1)}, f32[8,1,128]{2,1,0:T(1,128)}, u32[]{:S(2)}) copy-start(f32[8,1,128]{2,1,0:T(1,128)} %param.22) | copy-start | bytes 12292
  6.0 13.9 %copy-start.14 = (f32[8]{0:T(128)S(1)}, f32[8]{0:T(128)}, u32[]{:S(2)}) copy-start(f32[8]{0:T(128)} %param.23) | copy-start | bytes 100
  6.0 14.3 %copy-start.9 = (f32[2,8,1,16]{3,1,2,0:T(8,128)S(1)}, f32[2,8,1,16]{3,1,2,0:T(8,128)}, u32[]{:S(2)}) copy-start(f32[2,8,1,16]{3,1,2,0:T(8,128)} %constant.441.clone.1) | copy-start | bytes 3076
  6.0 14.5 %copy-start.4 = (f32[2,8,16]{2,1,0:T(8,128)S(1)}, f32[2,8,16]{2,1,0:T(8,128)}, u32[]{:S(2)}) copy-start(f32[2,8,16]{2,1,0:T(8,128)} %constant.448.clone.1) | copy-start | bytes 3076
  14.2 46.1 %all-to-all-start = ((f32[8,1,32768]{2,1,0:T(1,128)}), f32[8,1,32768]{2,1,0:T(1,128)S(1)}, u32[]{:S(2)}, u32[]{:S(2)}) async-start(f32[8,1,32768]{2,1,0:T(1,128)} %reshape.3184), calls=%async_computation | async-start | bytes 2097152 | tf_op jit(solution)/shard_map/all_to_all | solution.py:168
  21.0 1.1 copy-start.8
  60.3 79.1 %all-to-all-start.2 = ((f32[4,2,192]{2,1,0:T(2,128)}), f32[4,2,192]{2,1,0:T(2,128)S(1)}, u32[]{:S(2)}, u32[]{:S(2)}) async-start(f32[4,2,192]{2,1,0:T(2,128)} %fusion.49), calls=%async_computation.2 | async-start | bytes 16384 | tf_op jit(solution)/shard_map/all_to_all | solution.py:113
  79.8 24.3 %slice-start = ((s8[8388608]{0:T(1024)(128)(4,1)}), s8[4194304]{0:T(1024)(128)(4,1)S(1)}, s32[]{:S(2)}) async-start(s8[8388608]{0:T(1024)(128)(4,1)} %bitcast.606), calls=%async_computation.5 | async-start | bytes 8388608
  91.6 12.5 %slice-start.1 = ((s8[8388608]{0:T(1024)(128)(4,1)}), s8[4194304]{0:T(1024)(128)(4,1)S(1)}, s32[]{:S(2)}) async-start(s8[8388608]{0:T(1024)(128)(4,1)} %bitcast.606), calls=%async_computation.6 | async-start | bytes 8388608
  139.4 20.0 %all-to-all-start.1 = ((f32[8,1,32768]{2,1,0:T(1,128)}), f32[8,1,32768]{2,1,0:T(1,128)S(1)}, u32[]{:S(2)}, u32[]{:S(2)}) async-start(f32[8,1,32768]{2,1,0:T(1,128)} %reshape.3186), calls=%async_computation.1 | async-start | bytes 2097152 | tf_op jit(solution)/shard_map/all_to_all | solution.py:172
  186.6 12.8 %copy-start.1 = (f32[8,8,128,1,1]{1,0,4,3,2:T(8,128)S(1)}, f32[8,8,128,1,1]{1,0,4,3,2:T(8,128)}, u32[]{:S(2)}) copy-start(f32[8,8,128,1,1]{1,0,4,3,2:T(8,128)} %copy.324) | copy-start | bytes 98308
  192.6 26.7 %collective-permute-start = (f32[2,8,8,16,1,128]{5,2,3,1,0,4:T(8,128)S(1)}, f32[2,8,8,16,1,128]{5,2,3,1,0,4:T(8,128)}, u32[]{:S(2)}, u32[]{:S(2)}) collective-permute-start(f32[2,8,8,16,1,128]{5,2,3,1,0,4:T(8,128)S(1)} %copy.285), channel_id=1, source_target_pairs={{1,0},{2,1},{3,2},{5,4},{6,5},{7,6},{9,8},{10,9},{11,10},{13,12},{... | collective-permute-start | bytes 3145736 | tf_op jit(solution)/shard_map/ppermute | solution.py:24
  193.9 25.5 %collective-permute-start.1 = (f32[2,8,8,16,1,128]{5,2,3,1,0,4:T(8,128)S(1)}, f32[2,8,8,16,1,128]{5,2,3,1,0,4:T(8,128)}, u32[]{:S(2)}, u32[]{:S(2)}) collective-permute-start(f32[2,8,8,16,1,128]{5,2,3,1,0,4:T(8,128)S(1)} %copy.285), channel_id=1, source_target_pairs={{0,1},{1,2},{2,3},{4,5},{5,6},{6,7},{8,9},{9,10},{10,11},{12,13},{... | collective-permute-start | bytes 3145736 | tf_op jit(solution)/shard_map/ppermute | solution.py:21
  218.6 1.2 copy-start.2
  271.9 24.3 %slice-start.2 = ((s8[8388608]{0:T(1024)(128)(4,1)}), s8[4194304]{0:T(1024)(128)(4,1)S(1)}, s32[]{:S(2)}) async-start(s8[8388608]{0:T(1024)(128)(4,1)} %bitcast.608), calls=%async_computation.7 | async-start | bytes 8388608
  283.8 12.5 %slice-start.3 = ((s8[8388608]{0:T(1024)(128)(4,1)}), s8[4194304]{0:T(1024)(128)(4,1)S(1)}, s32[]{:S(2)}) async-start(s8[8388608]{0:T(1024)(128)(4,1)} %bitcast.608), calls=%async_computation.8 | async-start | bytes 8388608
  382.6 8.4 %copy-start.12 = (f32[2,8,1,1]{1,0,3,2:T(2,128)S(1)}, f32[2,8,1,1]{1,0,3,2:T(2,128)}, u32[]{:S(2)}) copy-start(f32[2,8,1,1]{1,0,3,2:T(2,128)} %constant.549) | copy-start | bytes 196
  400.8 6.9 %copy-start.10 = (f32[4,8,1]{1,0,2:T(4,128)S(1)}, f32[4,8,1]{1,0,2:T(4,128)}, u32[]{:S(2)}) copy-start(f32[4,8,1]{1,0,2:T(4,128)} %constant.551) | copy-start | bytes 388
  400.8 7.3 %copy-start.6 = (f32[4,8,1]{1,0,2:T(4,128)S(1)}, f32[4,8,1]{1,0,2:T(4,128)}, u32[]{:S(2)}) copy-start(f32[4,8,1]{1,0,2:T(4,128)} %constant.552) | copy-start | bytes 388
  400.8 49.5 %copy-start.11 = (f32[2,8,1,1]{1,0,3,2:T(2,128)S(1)}, f32[2,8,1,1]{1,0,3,2:T(2,128)}, u32[]{:S(2)}) copy-start(f32[2,8,1,1]{1,0,3,2:T(2,128)} %constant.550) | copy-start | bytes 196
where the time goes:
time: 461 us; the launch traced here: 453 us
  local copies, waits for them, and re-layouts  191 us (41%)
  matrix products  111 us (24%)
  blocking collectives  78.9 us (17%)
  other arithmetic  34.3 us (7%)
  starting transfers between devices  22 us (5%)
  waiting for transfers between devices  13.6 us (3%)
    dot_general x8, matrix products, contract(): jnp.einsum('tsmbyx,tbpmyx->tbpsyx', former, latter, precision=HIGHEST)  89.9 us
    unnamed x62, local copies, waits for them, and re-layouts  73.5 us
    psum x1, blocking collectives, on_device(): projected = lax.psum(projected * scale, ('cuts', 'tile'))  41.1 us
    squeeze x4, local copies, waits for them, and re-layouts, solve(): return back_home[:, :, :, :, 0]  23.3 us
    gather x16, local copies, waits for them, and re-layouts, line_kernel(): return jnp.take(profile, jnp.asarray(offsets, dtype=jnp.int32), axis=1)  23.2 us
    all_to_all x1, blocking collectives, solve(): lax.all_to_all(residual[:, :, :, :, None], 'cuts', split_axis=6, concat_a...  18.9 us
    all_to_all x1, blocking collectives, solve(): lax.all_to_all(spread, 'cuts', split_axis=4, concat_axis=6, tiled=True)  18.9 us
    add x2, local copies, waits for them, and re-layouts, on_device(): first_step + solver(couple_cells(first_step, cross_hop, strain_mix))  14.5 us
  transfers between devices with their start and end apart: 5, of which 1 were waited for; matrix products, arithmetic and copies ran while one was open for 30% of the time, Pallas kernels for 0%

commit v1 on v0

v1 whole, which is shorter than its diff:
```python
import functools
import math

import jax
import jax.numpy as jnp
import numpy as np
from jax import lax
from jax.experimental import pallas as pl
from jax.experimental.pallas import tpu as pltpu
from jax.sharding import PartitionSpec as P

PTS = 8
HALF = PTS // 2
NMOM = 4
NFIELD = 2
MESH = pl.DeviceIdType.MESH

ANGLES = [math.pi * (2 * point + 1) / PTS for point in range(HALF)]


def line_green(edge, hop, length):
    half = length // 2
    parts = []
    for angle in ANGLES:
        zr, zi = math.cos(angle), math.sin(angle)
        modes = []
        for k in range(half + 1):
            shifted = (zr - edge) + (2.0 * math.cos(2 * math.pi * k / length)) * hop
            inverse = 1.0 / (shifted * shifted + zi * zi)
            modes.append((shifted * inverse, (-zi) * inverse))
        for comp in range(2):
            rows = []
            for d in range(half + 1):
                total = None
                for k in range(half + 1):
                    weight = (1.0 if k in (0, half) else 2.0) / length
                    term = modes[k][comp] * (weight * math.cos(2 * math.pi * k * d / length))
                    total = term if total is None else total + term
                rows.append(total)
            parts.append(rows)
    return parts


def kernel(
    dims,
    ids_ref,
    hop_ref,
    cross_ref,
    deform_ref,
    probe_ref,
    test_ref,
    edge_ref,
    elastic_ref,
    field_ref,
    proj_ref,
    slots,
    send,
    got,
    edges,
    green,
    mixer,
    first,
    second,
    back,
    home,
    final,
    part,
    part_tile,
    part_cut,
    send_sem,
    got_sem,
    edge_send,
    edge_sem,
    back_send,
    home_sem,
    tile_send,
    tile_sem,
    cut_send,
    cut_sem,
):
    S, T, B, R, X, NS, SC = dims
    W = min(S, R)
    npr = R // W
    half = S // 2
    D = half + 1
    F = 2 * HALF
    chunk = npr * B
    msg = chunk + 8
    ret = NMOM * chunk
    N = S * T
    cut = lax.axis_index("cuts")
    tile = lax.axis_index("tile")
    me = cut * T + tile

    barrier = pltpu.get_barrier_semaphore()

    def greet(off, carry):
        other = lax.rem(me + off, N)
        pl.semaphore_signal(
            barrier, inc=1, device_id=(other // T, lax.rem(other, T)), device_id_type=MESH
        )
        return carry

    lax.fori_loop(1, N, greet, 0)

    slots[...] = jnp.zeros_like(slots)
    for i in range(NS):
        slots[0:6, i * SC : (i + 1) * SC] = elastic_ref[i]
    held = slots[...]
    turned = [held] + [pltpu.roll(held, SC * d, 1) for d in range(1, NS)]
    lane = lax.broadcasted_iota(jnp.int32, (8, X), 1)
    group = lane // SC
    own_ids = [ids_ref[tile * NS + i] for i in range(NS)]
    for t in range(T):
        placed = jnp.zeros((8, X), jnp.float32)
        for i in range(NS):
            for g in range(NS):
                wanted = jnp.where(group == g, t * NS + g, -1)
                placed = jnp.where(wanted == own_ids[i], turned[(g - i) % NS], placed)
        for w in range(W):
            row = (t * W + w) * msg
            for i in range(npr):
                send[row + i * B : row + (i + 1) * B, :] = probe_ref[
                    pl.ds(w * npr + i, B, stride=R), :
                ]
            send[row + chunk : row + msg, :] = placed
    edges[1] = edge_ref[...]

    pl.semaphore_wait(barrier, N - 1)

    def message(target_tile, target_cut, off, near):
        source = (target_tile * W + lax.rem(target_cut, W)) * msg
        landing = (tile * S + cut) * msg
        skip = 0 if near else chunk
        return pltpu.make_async_remote_copy(
            src_ref=send.at[pl.ds(pl.multiple_of(source + skip, 8), msg - skip), :],
            dst_ref=got.at[pl.ds(pl.multiple_of(landing + skip, 8), msg - skip), :],
            send_sem=send_sem.at[off],
            recv_sem=got_sem.at[tile, cut],
            device_id=(target_cut, target_tile),
            device_id_type=MESH,
        )

    def edge_copy(side):
        return pltpu.make_async_remote_copy(
            src_ref=edge_ref,
            dst_ref=edges.at[2 - side],
            send_sem=edge_send.at[side],
            recv_sem=edge_sem.at[2 - side],
            device_id=(cut, tile + side - 1),
            device_id_type=MESH,
        )

    has_side = {0: tile > 0, 2: tile < T - 1}
    for side in (0, 2):
        pl.when(has_side[side])(lambda side=side: edge_copy(side).start())

    def each_other(act):
        def body(off, carry):
            other = lax.rem(me + off, N)
            there_cut, there_tile = other // T, lax.rem(other, T)
            near = jnp.abs(there_tile - tile) <= 1

            @pl.when(near)
            def _():
                act(there_tile, there_cut, off, True)

            @pl.when(jnp.logical_not(near))
            def _():
                act(there_tile, there_cut, off, False)

            return carry

        lax.fori_loop(1, N, body, 0)

    each_other(lambda t, c, off, near: message(t, c, off, near).start())
    here = pl.multiple_of((tile * S + cut) * msg, 8)
    mine = pl.multiple_of((tile * W + lax.rem(cut, W)) * msg, 8)
    got[pl.ds(here, msg), :] = send[pl.ds(mine, msg), :]

    band = lax.broadcasted_iota(jnp.int32, (B, X), 0)
    hop = jnp.zeros((B, X), jnp.float32)
    for b in range(B):
        hop = jnp.where(band == b, hop_ref[b], hop)

    def fill_green(row):
        parts = line_green(edges[row], hop, S)
        for f in range(F):
            for d in range(D):
                green[row, f * D + d] = parts[f][d]
        return parts

    parts = fill_green(1)
    for p in range(NMOM):
        for j in range(HALF):
            wr = 2.0 * math.cos((p + 1) * ANGLES[j]) / PTS
            wi = 2.0 * math.sin((p + 1) * ANGLES[j]) / PTS
            for d in range(D):
                re, im = parts[2 * j][d], parts[2 * j + 1][d]
                final[(p * D + d) * F + 2 * j] = wr * re - wi * im
                final[(p * D + d) * F + 2 * j + 1] = -(wr * im + wi * re)
    for side in (0, 2):

        @pl.when(has_side[side])
        def _(side=side):
            edge_copy(2 - side).wait_recv()
            fill_green(side)

    def arrived(t, c, off, near):
        skip = 0 if near else chunk
        place = got.at[pl.ds(pl.multiple_of((t * S + c) * msg + skip, 8), msg - skip), :]
        pltpu.make_async_remote_copy(
            src_ref=place,
            dst_ref=place,
            send_sem=send_sem.at[off],
            recv_sem=got_sem.at[t, c],
            device_id=(c, t),
            device_id_type=MESH,
        ).wait_recv()

    each_other(arrived)

    def solve_row(row):
        base = (tile + row - 1) * (S * msg)

        def body(b, carry):
            for i in range(npr):
                line = got[pl.ds(base + i * B + b, S, stride=msg), :]
                sums = [line]
                for d in range(1, half):
                    sums.append(pltpu.roll(line, d, 0) + pltpu.roll(line, S - d, 0))
                sums.append(pltpu.roll(line, half, 0))
                for f in range(F):
                    total = None
                    for d in range(D):
                        term = green[row, f * D + d, pl.ds(b, 1), :] * sums[d]
                        total = term if total is None else total + term
                    first[row, b, f * npr + i] = total
            return carry

        lax.fori_loop(0, B, body, 0)

    solve_row(1)
    for side in (0, 2):
        pl.when(has_side[side])(lambda side=side: solve_row(side))

        @pl.when(jnp.logical_not(has_side[side]))
        def _(side=side):
            def clear(b, carry):
                first[side, b] = jnp.zeros_like(first[side, 0])
                return carry

            lax.fori_loop(0, B, clear, 0)

    strain = []
    for k in range(6):
        total = None
        for t in range(T):
            term = got[pl.ds(t * S * msg + chunk + k, S, stride=msg), :]
            total = term if total is None else total + term
        strain.append(total)
    for b in range(B):
        for c in range(b, B):
            total = None
            for k in range(6):
                term = (0.5 * (deform_ref[k, b, c] + deform_ref[k, c, b])) * strain[k]
                total = term if total is None else total + term
            mixer[b, c] = total
            if c != b:
                mixer[c, b] = total

    lanes = lax.broadcasted_iota(jnp.int32, (1, 1, X), 2)
    block = max(1, 8 * 8 // S)
    pieces = F * npr // block

    def couple(step, carry):
        b, piece = step // pieces, lax.rem(step, pieces)
        pick = pl.ds(piece * block, block)
        right = left = stay = None
        for c in range(B):
            u = first[1, c, pick]
            up, down = first[2, c, pick], first[0, c, pick]
            a = cross_ref[0, b, c] * u
            l = cross_ref[0, c, b] * u
            s = mixer[b, c][None] * u + cross_ref[1, b, c] * up + cross_ref[1, c, b] * down
            right = a if right is None else right + a
            left = l if left is None else left + l
            stay = s if stay is None else stay + s
        flat = (block * S, X)
        right = pltpu.roll(right.reshape(flat), X - 1, 1).reshape(block, S, X)
        left = pltpu.roll(left.reshape(flat), 1, 1).reshape(block, S, X)
        stay = stay + jnp.where(lanes < X - 1, right, 0.0) + jnp.where(lanes > 0, left, 0.0)
        second[b, pick] = stay
        return carry

    lax.fori_loop(0, B * pieces, couple, 0)

    def moments(b, carry):
        for i in range(npr):
            ys = [second[b, f * npr + i] for f in range(F)]
            xs = [first[1, b, f * npr + i] for f in range(F)]
            for p in range(NMOM):
                total = None
                for j in range(HALF):
                    wr = 2.0 * math.cos((p + 1) * ANGLES[j]) / PTS
                    wi = 2.0 * math.sin((p + 1) * ANGLES[j]) / PTS
                    term = wr * xs[2 * j] - wi * xs[2 * j + 1]
                    total = term if total is None else total + term
                for d in range(D):
                    z = None
                    for f in range(F):
                        term = final[(p * D + d) * F + f, pl.ds(b, 1), :] * ys[f]
                        z = term if z is None else z + term
                    if d == 0:
                        total = total + z
                    elif d == half:
                        total = total + pltpu.roll(z, half, 0)
                    else:
                        total = total + pltpu.roll(z, d, 0) + pltpu.roll(z, S - d, 0)
                back[pl.ds((p * npr + i) * B + b, S, stride=ret), :] = total
        return carry

    lax.fori_loop(0, B, moments, 0)

    mates = (cut // W) * W
    rank = lax.rem(cut, W)

    def home_copy(off, inbound):
        other = lax.rem(rank + off, W)
        source = pl.multiple_of((mates + other) * ret, 8)
        landing = pl.multiple_of((other if inbound else rank) * ret, 8)
        return pltpu.make_async_remote_copy(
            src_ref=back.at[pl.ds(source, ret), :],
            dst_ref=home.at[pl.ds(landing, ret), :],
            send_sem=back_send.at[off],
            recv_sem=home_sem.at[other if inbound else rank],
            device_id=(mates + other, tile),
            device_id_type=MESH,
        )

    def run(low, high, act):
        def body(off, carry):
            act(off)
            return carry

        lax.fori_loop(low, high, body, 0)

    run(1, W, lambda off: home_copy(off, False).start())
    home[pl.ds(pl.multiple_of(rank * ret, 8), ret), :] = back[
        pl.ds(pl.multiple_of(cut * ret, 8), ret), :
    ]
    run(1, W, lambda off: home_copy(off, True).wait_recv())

    acc = None
    for b in range(B):
        rows = home[pl.ds(b, W * NMOM * npr, stride=B), :]
        term = lax.dot_general(
            test_ref[b * R : (b + 1) * R, :],
            rows,
            (((1,), (1,)), ((), ())),
            precision=lax.Precision.HIGHEST,
            preferred_element_type=jnp.float32,
        )
        acc = term if acc is None else acc + term
    scale = (S * B * T * X) ** (-0.5)
    part_tile[tile] = jnp.zeros_like(part)
    part_tile[tile, :, : NMOM * R] = acc * scale

    def tile_copy(off, inbound):
        other = lax.rem(tile + off, T)
        return pltpu.make_async_remote_copy(
            src_ref=part_tile.at[tile],
            dst_ref=part_tile.at[other if inbound else tile],
            send_sem=tile_send.at[off],
            recv_sem=tile_sem.at[other if inbound else tile],
            device_id=(cut, other),
            device_id_type=MESH,
        )

    def cut_copy(off, inbound):
        other = lax.rem(cut + off, S)
        return pltpu.make_async_remote_copy(
            src_ref=part_cut.at[cut],
            dst_ref=part_cut.at[other if inbound else cut],
            send_sem=cut_send.at[off],
            recv_sem=cut_sem.at[other if inbound else cut],
            device_id=(other, tile),
            device_id_type=MESH,
        )

    run(1, T, lambda off: tile_copy(off, False).start())
    for w in range(W):
        for p in range(NFIELD):
            for i in range(npr):
                row = w * ret + (p * npr + i) * B
                field_ref[pl.ds(p * B * R + w * npr + i, B, stride=R), :] = home[row : row + B, :]
    run(1, T, lambda off: tile_copy(off, True).wait_recv())
    total = part_tile[0]
    for t in range(1, T):
        total = total + part_tile[t]
    part_cut[cut] = total
    run(1, S, lambda off: cut_copy(off, False).start())

    each_other(lambda t, c, off, near: message(t, c, off, near).wait_send())
    for side in (0, 2):
        pl.when(has_side[side])(lambda side=side: edge_copy(side).wait_send())
    run(1, W, lambda off: home_copy(off, False).wait_send())
    run(1, T, lambda off: tile_copy(off, False).wait_send())
    run(1, S, lambda off: cut_copy(off, True).wait_recv())
    total = part_cut[0]
    for c in range(1, S):
        total = total + part_cut[c]
    proj_ref[...] = total
    run(1, S, lambda off: cut_copy(off, False).wait_send())


def on_device(
    S, T, probes, test_block, band_edge, slice_hop, cross_hop, deform, strain_elastic, strain_ids
):
    _, B, R, _, X = probes.shape
    NS, SC = strain_elastic.shape[1], strain_elastic.shape[3]
    dims = (S, T, B, R, X, NS, SC)
    W = min(S, R)
    npr = R // W
    D = S // 2 + 1
    F = 2 * HALF
    chunk = npr * B
    msg = chunk + 8
    ret = NMOM * chunk
    smem = pl.BlockSpec(memory_space=pltpu.SMEM)
    vmem = pl.BlockSpec(memory_space=pltpu.VMEM)
    f32 = jnp.float32
    dma = pltpu.SemaphoreType.DMA
    fields, proj = pl.pallas_call(
        functools.partial(kernel, dims),
        out_shape=(
            jax.ShapeDtypeStruct((NFIELD * B * R, X), f32),
            jax.ShapeDtypeStruct((R, X), f32),
        ),
        in_specs=[smem] * 4 + [vmem] * 4,
        out_specs=(vmem, vmem),
        scratch_shapes=[
            pltpu.VMEM((8, X), f32),
            pltpu.VMEM((T * W * msg, X), f32),
            pltpu.VMEM((T * S * msg, X), f32),
            pltpu.VMEM((3, B, X), f32),
            pltpu.VMEM((3, F * D, B, X), f32),
            pltpu.VMEM((B, B, S, X), f32),
            pltpu.VMEM((3, B, F * npr, S, X), f32),
            pltpu.VMEM((B, F * npr, S, X), f32),
            pltpu.VMEM((S * ret, X), f32),
            pltpu.VMEM((W * ret, X), f32),
            pltpu.VMEM((NMOM * D * F, B, X), f32),
            pltpu.VMEM((R, X), f32),
            pltpu.VMEM((T, R, X), f32),
            pltpu.VMEM((S, R, X), f32),
            dma((S * T,)),
            dma((T, S)),
            dma((3,)),
            dma((3,)),
            dma((W,)),
            dma((W,)),
            dma((T,)),
            dma((T,)),
            dma((S,)),
            dma((S,)),
        ],
        compiler_params=pltpu.CompilerParams(
            collective_id=0, has_side_effects=True, vmem_limit_bytes=48 * 1024 * 1024
        ),
    )(
        strain_ids,
        slice_hop,
        cross_hop,
        deform,
        probes.reshape(B * R, X),
        test_block.reshape(B * R, X),
        band_edge.reshape(B, X),
        strain_elastic[0],
    )
    fields = fields.reshape(NFIELD, 1, 1, B, R, 1, X)
    fields = jnp.concatenate([fields, jnp.zeros_like(fields)], axis=1)
    proj = proj[:, : NMOM * R].reshape(R, W, NMOM, npr)
    proj = jnp.transpose(proj, (2, 0, 1, 3)).reshape(NMOM, 1, R, R)
    return fields, jnp.concatenate([proj, jnp.zeros_like(proj)], axis=1)


def solution(mesh):
    placed = (
        P("cuts", None, None, "tile", None),
        P("cuts", None, None, "tile", None),
        P(None, "tile", None),
        P(),
        P(),
        P(),
        P("cuts", "tile", None, None),
        P(),
    )
    return jax.shard_map(
        functools.partial(on_device, mesh.shape["cuts"], mesh.shape["tile"]),
        mesh=mesh,
        in_specs=placed,
        out_specs=(P(None, None, "cuts", None, None, "tile", None), P()),
        check_vma=False,
    )
```

time: 461 us -> 38.4 us (0.08); the launches traced: 453 us -> 38.1 us
  local copies, waits for them, and re-layouts: 191 us -> 5.41 us
  matrix products: 111 us -> 0 us
  blocking collectives: 78.9 us -> 0 us
  other arithmetic: 34.3 us -> 0 us
  Pallas kernels: 0 us -> 32 us
  starting transfers between devices: 22 us -> 0 us
  waiting for transfers between devices: 13.6 us -> 0 us
    dot_general x23 -> x0, matrix products: 111 us -> none  [the longest x8 89.9 us: contract(): jnp.einsum('tsmbyx,tbpmyx->tbpsyx', former, latter, precision=HIGHEST)]
    unnamed x62 -> x16, local copies, waits for them, and re-layouts: 73.5 us -> 3.82 us
    psum x1 -> x0, blocking collectives: 41.1 us -> none  [on_device(): projected = lax.psum(projected * scale, ('cuts', 'tile'))]
    all_to_all x2 -> x0, blocking collectives: 37.8 us -> none  [the longest x1 18.9 us: solve(): lax.all_to_all(residual[:, :, :, :, None], 'cuts', split_axis=6, concat_a...]
    pallas_call x0 -> x1, Pallas kernels: none -> 32 us  [on_device(): pl.pallas_call(functools.partial(kernel, dims), out_shape=(jax.ShapeDtype...]
    squeeze x7 -> x0, local copies, waits for them, and re-layouts: 23.5 us -> none  [the longest x4 23.3 us: solve(): return back_home[:, :, :, :, 0]]
    gather x16 -> x0, local copies, waits for them, and re-layouts: 23.2 us -> none  [line_kernel(): return jnp.take(profile, jnp.asarray(offsets, dtype=jnp.int32), axis=1)]
    another operation x10 -> x0, local copies, waits for them, and re-layouts: 22 us -> none  [the longest x2 9.72 us: lines(): jnp.stack([contract(kernel[0], received[0]) - contract(kernel[1], receive...]
  transfers between devices with their start and end apart: 5 -> 0, of which waited for: 1 -> 0; matrix products, arithmetic and copies ran while one was open for 30% -> 0% of each run, Pallas kernels for 0% -> 0%
where the time goes in v1:
time: 38.4 us; the launch traced here: 38.1 us
  Pallas kernels  32 us (83%)
  local copies, waits for them, and re-layouts  5.41 us (14%)
  between operations  0.68 us (2%)
    pallas_call x1, Pallas kernels, on_device(): pl.pallas_call(functools.partial(kernel, dims), out_shape=(jax.ShapeDtype...  32 us
    unnamed x16, local copies, waits for them, and re-layouts  3.82 us
    concatenate x1, local copies, waits for them, and re-layouts, on_device(): fields = jnp.concatenate([fields, jnp.zeros_like(fields)], axis=1)  0.85 us

profile of v1, /device:TPU:0, one launch (start us, length us, event | category | flops | bytes accessed | tf_op | source)
XLA Modules:
  0.0 38.1 jit_solution(8451113132535934889)
XLA Ops:
  0.6 0.0 copy-start.2
  0.6 0.0 copy-start.3
  0.7 0.7 %copy.20 = f32[1,4,6,32]{3,2,1,0:T(8,128)S(1)} copy(f32[1,4,6,32]{3,1,2,0:T(4,128)} %param.14) | data formatting | bytes 6144 | tf_op args[6]
  1.4 0.0 copy-start.5
  1.4 0.0 copy-start.6
  1.4 0.0 copy-done.2
  1.4 0.0 copy-done.3
  1.4 0.6 %copy-done.5 = s32[16]{0:T(128)S(1)} copy-done((s32[16]{0:T(128)S(1)}, s32[16]{0:T(128)}, u32[]{:S(2)}) %copy-start.5) | copy-done | bytes 88
  2.0 0.0 copy-done.6
  2.0 0.0 copy-start
  2.0 0.8 %copy-done = f32[1,8,16,1,128]{4,3,2,1,0:T(1,128)S(1)} copy-done((f32[1,8,16,1,128]{4,3,2,1,0:T(1,128)S(1)}, f32[1,8,16,1,128]{4,3,2,1,0:T(1,128)}, u32[]{:S(2)}) %copy-start) | copy-done | bytes 65560
  2.9 0.0 copy-start.1
  2.9 0.8 %copy-done.1 = f32[1,8,16,1,128]{4,3,2,1,0:T(1,128)S(1)} copy-done((f32[1,8,16,1,128]{4,3,2,1,0:T(1,128)S(1)}, f32[1,8,16,1,128]{4,3,2,1,0:T(1,128)}, u32[]{:S(2)}) %copy-start.1) | copy-done | bytes 65560
  3.7 0.0 copy-start.4
  3.7 0.7 %copy-done.4 = f32[8,1,128]{2,1,0:T(1,128)S(1)} copy-done((f32[8,1,128]{2,1,0:T(1,128)S(1)}, f32[8,1,128]{2,1,0:T(1,128)}, u32[]{:S(2)}) %copy-start.4) | copy-done | bytes 4120
  4.4 32.0 %shard_map.95 = (f32[256,128]{1,0:T(8,128)S(1)}, f32[16,128]{1,0:T(8,128)S(1)}) custom-call(s32[16]{0:T(128)S(1)} %copy-done.5, f32[8]{0:T(128)S(1)} %copy-done.6, f32[2,8,8]{2,1,0:T(8,128)S(1)} %copy-done.3, f32[6,8,8]{2,1,0:T(8,128)S(1)} %copy-done.2, f32[128,128]{1,0:T(8,128)S(1)} %bitcast.15, f32[128,128]{1,0:T(8,128)S(1)} %bitcast.16, ...), custom_call_target="tpu_custom_call" | custom-call | tf_op jit(solution)/shard_map/pallas_call | solution.py:434
  36.4 0.9 %concatenate.6 = f32[2,2,1,8,16,1,128]{6,5,4,3,2,1,0:T(1,128)} pad(f32[2,1,1,8,16,1,128]{6,5,4,3,2,1,0:T(1,128)S(1)} %bitcast.14, f32[]{:T(128)} %constant.1.clone.1), padding=0_0x0_1x0_0x0_0x0_0x0_0x0_0 | pad | bytes 393220 | tf_op jit(solution)/shard_map/concatenate | solution.py:482
  37.2 0.1 copy.15
  37.3 0.1 copy.18
  37.4 0.6 %concatenate.7.clone = f32[4,2,16,16]{3,2,1,0:T(8,128)} pad(f32[4,1,16,16]{3,2,1,0:T(8,128)S(1)} %copy.18, f32[]{:T(128)} %constant.1.clone.1), padding=0_0x0_1x0_0x0_0 | pad | bytes 12292 | tf_op jit(solution)/shard_map/concatenate | solution.py:485
  (1 shorter events, 0.0 us)
Async XLA Ops:
  0.6 0.7 %copy-start.2 = (f32[6,8,8]{2,1,0:T(8,128)S(1)}, f32[6,8,8]{2,1,0:T(8,128)}, u32[]{:S(2)}) copy-start(f32[6,8,8]{2,1,0:T(8,128)} %deform_ref.1) | copy-start | bytes 4612
  0.6 0.7 %copy-start.3 = (f32[2,8,8]{2,1,0:T(8,128)S(1)}, f32[2,8,8]{2,1,0:T(8,128)}, u32[]{:S(2)}) copy-start(f32[2,8,8]{2,1,0:T(8,128)} %cross_ref.1) | copy-start | bytes 1540
  1.4 0.7 %copy-start.5 = (s32[16]{0:T(128)S(1)}, s32[16]{0:T(128)}, u32[]{:S(2)}) copy-start(s32[16]{0:T(128)} %ids_ref.1) | copy-start | bytes 196
  1.4 0.7 %copy-start.6 = (f32[8]{0:T(128)S(1)}, f32[8]{0:T(128)}, u32[]{:S(2)}) copy-start(f32[8]{0:T(128)} %hop_ref.1) | copy-start | bytes 100
  2.0 0.8 %copy-start = (f32[1,8,16,1,128]{4,3,2,1,0:T(1,128)S(1)}, f32[1,8,16,1,128]{4,3,2,1,0:T(1,128)}, u32[]{:S(2)}) copy-start(f32[1,8,16,1,128]{4,3,2,1,0:T(1,128)} %param.8) | copy-start | bytes 196612
  2.9 0.8 %copy-start.1 = (f32[1,8,16,1,128]{4,3,2,1,0:T(1,128)S(1)}, f32[1,8,16,1,128]{4,3,2,1,0:T(1,128)}, u32[]{:S(2)}) copy-start(f32[1,8,16,1,128]{4,3,2,1,0:T(1,128)} %param.9) | copy-start | bytes 196612
  3.7 0.7 %copy-start.4 = (f32[8,1,128]{2,1,0:T(1,128)S(1)}, f32[8,1,128]{2,1,0:T(1,128)}, u32[]{:S(2)}) copy-start(f32[8,1,128]{2,1,0:T(1,128)} %param.10) | copy-start | bytes 12292

commit v2 on v1

--- a/solution.py
+++ b/solution.py
@@ -43,16 +43,23 @@
 
 def kernel(
     dims,
+    ids_in,
+    hop_in,
+    cross_in,
+    deform_in,
+    probe_in,
+    test_in,
+    edge_in,
+    elastic_in,
+    field_ref,
+    proj_ref,
     ids_ref,
     hop_ref,
     cross_ref,
     deform_ref,
     probe_ref,
-    test_ref,
-    edge_ref,
     elastic_ref,
-    field_ref,
-    proj_ref,
+    tests,
     slots,
     send,
     got,
@@ -64,19 +71,18 @@
     back,
     home,
     final,
-    part,
-    part_tile,
-    part_cut,
+    parts_all,
+    load_sem,
     send_sem,
     got_sem,
     edge_send,
     edge_sem,
     back_send,
     home_sem,
-    tile_send,
-    tile_sem,
-    cut_send,
-    cut_sem,
+    test_send,
+    test_sem,
+    part_send,
+    part_sem,
 ):
     S, T, B, R, X, NS, SC = dims
     W = min(S, R)
@@ -87,11 +93,30 @@
     chunk = npr * B
     msg = chunk + 8
     ret = NMOM * chunk
+    kept = NFIELD * chunk
     N = S * T
     cut = lax.axis_index("cuts")
     tile = lax.axis_index("tile")
     me = cut * T + tile
 
+    own_tests = pl.ds(pl.multiple_of(cut * (B * R), 8), B * R)
+    loads = [
+        pltpu.make_async_copy(src, dst, load_sem.at[n])
+        for n, (src, dst) in enumerate(
+            (
+                (probe_in, probe_ref),
+                (elastic_in, elastic_ref),
+                (ids_in, ids_ref),
+                (edge_in, edges.at[1]),
+                (hop_in, hop_ref),
+                (cross_in, cross_ref),
+                (deform_in, deform_ref),
+                (test_in, tests.at[own_tests, :]),
+            )
+        )
+    ]
+    for load in loads:
+        load.start()
     barrier = pltpu.get_barrier_semaphore()
 
     def greet(off, carry):
@@ -104,8 +129,11 @@
     lax.fori_loop(1, N, greet, 0)
 
     slots[...] = jnp.zeros_like(slots)
-    for i in range(NS):
-        slots[0:6, i * SC : (i + 1) * SC] = elastic_ref[i]
+    for load in loads[:3]:
+        load.wait()
+    for k in range(6):
+        for i in range(NS):
+            slots[k : k + 1, i * SC : (i + 1) * SC] = elastic_ref[k, i : i + 1, :]
     held = slots[...]
     turned = [held] + [pltpu.roll(held, SC * d, 1) for d in range(1, NS)]
     lane = lax.broadcasted_iota(jnp.int32, (8, X), 1)
@@ -124,7 +152,8 @@
                     pl.ds(w * npr + i, B, stride=R), :
                 ]
             send[row + chunk : row + msg, :] = placed
-    edges[1] = edge_ref[...]
+    for load in loads[3:]:
+        load.wait()
 
     pl.semaphore_wait(barrier, N - 1)
 
@@ -143,7 +172,7 @@
 
     def edge_copy(side):
         return pltpu.make_async_remote_copy(
-            src_ref=edge_ref,
+            src_ref=edges.at[1],
             dst_ref=edges.at[2 - side],
             send_sem=edge_send.at[side],
             recv_sem=edge_sem.at[2 - side],
@@ -220,22 +249,48 @@
 
     each_other(arrived)
 
+    def run(low, high, act):
+        def body(off, carry):
+            act(off)
+            return carry
+
+        lax.fori_loop(low, high, body, 0)
+
+    def test_copy(off, inbound):
+        other = lax.rem(cut + off, S)
+        landing = pl.multiple_of((other if inbound else cut) * (B * R), 8)
+        return pltpu.make_async_remote_copy(
+            src_ref=tests.at[own_tests, :],
+            dst_ref=tests.at[pl.ds(landing, B * R), :],
+            send_sem=test_send.at[off],
+            recv_sem=test_sem.at[other if inbound else cut],
+            device_id=(other, tile),
+            device_id_type=MESH,
+        )
+
+    run(1, S, lambda off: test_copy(off, False).start())
+
     def solve_row(row):
         base = (tile + row - 1) * (S * msg)
 
         def body(b, carry):
+            sums = []
             for i in range(npr):
                 line = got[pl.ds(base + i * B + b, S, stride=msg), :]
-                sums = [line]
+                pairs = [line]
                 for d in range(1, half):
-                    sums.append(pltpu.roll(line, d, 0) + pltpu.roll(line, S - d, 0))
-                sums.append(pltpu.roll(line, half, 0))
-                for f in range(F):
-                    total = None
-                    for d in range(D):
-                        term = green[row, f * D + d, pl.ds(b, 1), :] * sums[d]
-                        total = term if total is None else total + term
-                    first[row, b, f * npr + i] = total
+                    pairs.append(pltpu.roll(line, d, 0) + pltpu.roll(line, S - d, 0))
+                pairs.append(pltpu.roll(line, half, 0))
+                sums.append(pairs)
+            for f in range(F):
+                totals = [None] * npr
+                for d in range(D):
+                    factor = green[row, f * D + d, pl.ds(b, 1), :]
+                    for i in range(npr):
+                        term = factor * sums[i][d]
+                        totals[i] = term if totals[i] is None else totals[i] + term
+                for i in range(npr):
+                    first[row, b, f * npr + i] = totals[i]
             return carry
 
         lax.fori_loop(0, B, body, 0)
@@ -296,28 +351,33 @@
     lax.fori_loop(0, B * pieces, couple, 0)
 
     def moments(b, carry):
-        for i in range(npr):
-            ys = [second[b, f * npr + i] for f in range(F)]
-            xs = [first[1, b, f * npr + i] for f in range(F)]
-            for p in range(NMOM):
-                total = None
-                for j in range(HALF):
-                    wr = 2.0 * math.cos((p + 1) * ANGLES[j]) / PTS
-                    wi = 2.0 * math.sin((p + 1) * ANGLES[j]) / PTS
-                    term = wr * xs[2 * j] - wi * xs[2 * j + 1]
-                    total = term if total is None else total + term
-                for d in range(D):
-                    z = None
-                    for f in range(F):
-                        term = final[(p * D + d) * F + f, pl.ds(b, 1), :] * ys[f]
-                        z = term if z is None else z + term
+        ys = [[second[b, f * npr + i] for f in range(F)] for i in range(npr)]
+        for p in range(NMOM):
+            totals = [None] * npr
+            for j in range(HALF):
+                wr = 2.0 * math.cos((p + 1) * ANGLES[j]) / PTS
+                wi = 2.0 * math.sin((p + 1) * ANGLES[j]) / PTS
+                for i in range(npr):
+                    re, im = (first[1, b, (2 * j + comp) * npr + i] for comp in range(2))
+                    term = wr * re - wi * im
+                    totals[i] = term if totals[i] is None else totals[i] + term
+            for d in range(D):
+                zs = [None] * npr
+                for f in range(F):
+                    factor = final[(p * D + d) * F + f, pl.ds(b, 1), :]
+                    for i in range(npr):
+                        term = factor * ys[i][f]
+                        zs[i] = term if zs[i] is None else zs[i] + term
+                for i in range(npr):
                     if d == 0:
-                        total = total + z
+                        totals[i] = totals[i] + zs[i]
                     elif d == half:
-                        total = total + pltpu.roll(z, half, 0)
+                        totals[i] = totals[i] + pltpu.roll(zs[i], half, 0)
                     else:
-                        total = total + pltpu.roll(z, d, 0) + pltpu.roll(z, S - d, 0)
-                back[pl.ds((p * npr + i) * B + b, S, stride=ret), :] = total
+                        turned_z = pltpu.roll(zs[i], d, 0) + pltpu.roll(zs[i], S - d, 0)
+                        totals[i] = totals[i] + turned_z
+            for i in range(npr):
+                back[pl.ds((p * npr + i) * B + b, S, stride=ret), :] = totals[i]
         return carry
 
     lax.fori_loop(0, B, moments, 0)
@@ -328,90 +388,83 @@
     def home_copy(off, inbound):
         other = lax.rem(rank + off, W)
         source = pl.multiple_of((mates + other) * ret, 8)
-        landing = pl.multiple_of((other if inbound else rank) * ret, 8)
+        landing = pl.multiple_of((other if inbound else rank) * kept, 8)
         return pltpu.make_async_remote_copy(
-            src_ref=back.at[pl.ds(source, ret), :],
-            dst_ref=home.at[pl.ds(landing, ret), :],
+            src_ref=back.at[pl.ds(source, kept), :],
+            dst_ref=home.at[pl.ds(landing, kept), :],
             send_sem=back_send.at[off],
             recv_sem=home_sem.at[other if inbound else rank],
             device_id=(mates + other, tile),
             device_id_type=MESH,
         )
 
-    def run(low, high, act):
-        def body(off, carry):
-            act(off)
-            return carry
-
-        lax.fori_loop(low, high, body, 0)
-
     run(1, W, lambda off: home_copy(off, False).start())
-    home[pl.ds(pl.multiple_of(rank * ret, 8), ret), :] = back[
-        pl.ds(pl.multiple_of(cut * ret, 8), ret), :
+    home[pl.ds(pl.multiple_of(rank * kept, 8), kept), :] = back[
+        pl.ds(pl.multiple_of(cut * ret, 8), kept), :
     ]
+
+    run(1, S, lambda off: test_copy(off, True).wait_recv())
+
+    def halves(values):
+        high = values.astype(jnp.bfloat16)
+        return high, (values - high.astype(jnp.float32)).astype(jnp.bfloat16)
+
+    def product(left, right):
+        return lax.dot_general(
+            left, right, (((1,), (1,)), ((), ())), preferred_element_type=jnp.float32
+        )
+
+    def project(s, acc):
+        high, low = halves(back[pl.ds(pl.multiple_of(s * ret, 8), ret), :])
+        test_high, test_low = halves(tests[pl.ds(pl.multiple_of(s * (B * R), 8), B * R), :])
+        small = product(high, test_low) + product(low, test_high)
+        return acc + (small + product(high, test_high))
+
+    acc = lax.fori_loop(0, S, project, jnp.zeros((ret, B * R), jnp.float32))
+    acc = acc.reshape(NMOM * npr, B, B * R)
+    lane_band = lax.broadcasted_iota(jnp.int32, acc.shape, 2) // R
+    same = lane_band == lax.broadcasted_iota(jnp.int32, acc.shape, 1)
+    acc = jnp.sum(jnp.where(same, acc, 0.0), axis=1)
+    total = acc
+    for b in range(1, B):
+        total = total + pltpu.roll(acc, b * R, 1)
+    lane_row = lax.broadcasted_iota(jnp.int32, total.shape, 1) // R
+    chosen = lane_row == lax.broadcasted_iota(jnp.int32, total.shape, 0)
+    total = jnp.sum(jnp.where(chosen, total, 0.0), axis=0, keepdims=True)
+    parts_all[me] = total * ((S * B * T * X) ** (-0.5))
+
+    def part_copy(off, inbound):
+        other = lax.rem(me + off, N)
+        return pltpu.make_async_remote_copy(
+            src_ref=parts_all.at[me],
+            dst_ref=parts_all.at[other if inbound else me],
+            send_sem=part_send.at[off],
+            recv_sem=part_sem.at[other if inbound else me],
+            device_id=(other // T, lax.rem(other, T)),
+            device_id_type=MESH,
+        )
+
+    run(1, N, lambda off: part_copy(off, False).start())
+
     run(1, W, lambda off: home_copy(off, True).wait_recv())
-
-    acc = None
-    for b in range(B):
-        rows = home[pl.ds(b, W * NMOM * npr, stride=B), :]
-        term = lax.dot_general(
-            test_ref[b * R : (b + 1) * R, :],
-            rows,
-            (((1,), (1,)), ((), ())),
-            precision=lax.Precision.HIGHEST,
-            preferred_element_type=jnp.float32,
-        )
-        acc = term if acc is None else acc + term
-    scale = (S * B * T * X) ** (-0.5)
-    part_tile[tile] = jnp.zeros_like(part)
-    part_tile[tile, :, : NMOM * R] = acc * scale
-
-    def tile_copy(off, inbound):
-        other = lax.rem(tile + off, T)
-        return pltpu.make_async_remote_copy(
-            src_ref=part_tile.at[tile],
-            dst_ref=part_tile.at[other if inbound else tile],
-            send_sem=tile_send.at[off],
-            recv_sem=tile_sem.at[other if inbound else tile],
-            device_id=(cut, other),
-            device_id_type=MESH,
-        )
-
-    def cut_copy(off, inbound):
-        other = lax.rem(cut + off, S)
-        return pltpu.make_async_remote_copy(
-            src_ref=part_cut.at[cut],
-            dst_ref=part_cut.at[other if inbound else cut],
-            send_sem=cut_send.at[off],
-            recv_sem=cut_sem.at[other if inbound else cut],
-            device_id=(other, tile),
-            device_id_type=MESH,
-        )
-
-    run(1, T, lambda off: tile_copy(off, False).start())
     for w in range(W):
         for p in range(NFIELD):
             for i in range(npr):
-                row = w * ret + (p * npr + i) * B
+                row = w * kept + (p * npr + i) * B
                 field_ref[pl.ds(p * B * R + w * npr + i, B, stride=R), :] = home[row : row + B, :]
-    run(1, T, lambda off: tile_copy(off, True).wait_recv())
-    total = part_tile[0]
-    for t in range(1, T):
-        total = total + part_tile[t]
-    part_cut[cut] = total
-    run(1, S, lambda off: cut_copy(off, False).start())
 
     each_other(lambda t, c, off, near: message(t, c, off, near).wait_send())
     for side in (0, 2):
         pl.when(has_side[side])(lambda side=side: edge_copy(side).wait_send())
+    run(1, S, lambda off: test_copy(off, False).wait_send())
     run(1, W, lambda off: home_copy(off, False).wait_send())
-    run(1, T, lambda off: tile_copy(off, False).wait_send())
-    run(1, S, lambda off: cut_copy(off, True).wait_recv())
-    total = part_cut[0]
-    for c in range(1, S):
-        total = total + part_cut[c]
-    proj_ref[...] = total
-    run(1, S, lambda off: cut_copy(off, False).wait_send())
+    run(1, N, lambda off: part_copy(off, True).wait_recv())
+    for w in range(W):
+        total = parts_all[w * T]
+        for t in range(1, T):
+            total = total + parts_all[w * T + t]
+        proj_ref[w : w + 1, :] = total
+    run(1, N, lambda off: part_copy(off, False).wait_send())
 
 
 def on_device(
@@ -427,7 +480,8 @@
     chunk = npr * B
     msg = chunk + 8
     ret = NMOM * chunk
-    smem = pl.BlockSpec(memory_space=pltpu.SMEM)
+    kept = NFIELD * chunk
+    hbm = pl.BlockSpec(memory_space=pltpu.HBM)
     vmem = pl.BlockSpec(memory_space=pltpu.VMEM)
     f32 = jnp.float32
     dma = pltpu.SemaphoreType.DMA
@@ -435,11 +489,18 @@
         functools.partial(kernel, dims),
         out_shape=(
             jax.ShapeDtypeStruct((NFIELD * B * R, X), f32),
-            jax.ShapeDtypeStruct((R, X), f32),
+            jax.ShapeDtypeStruct((W, B * R), f32),
         ),
-        in_specs=[smem] * 4 + [vmem] * 4,
+        in_specs=[hbm] * 8,
         out_specs=(vmem, vmem),
         scratch_shapes=[
+            pltpu.SMEM(strain_ids.shape, jnp.int32),
+            pltpu.SMEM(slice_hop.shape, f32),
+            pltpu.SMEM(cross_hop.shape, f32),
+            pltpu.SMEM(deform.shape, f32),
+            pltpu.VMEM((B * R, X), f32),
+            pltpu.VMEM((6, NS, SC), f32),
+            pltpu.VMEM((S * B * R, X), f32),
             pltpu.VMEM((8, X), f32),
             pltpu.VMEM((T * W * msg, X), f32),
             pltpu.VMEM((T * S * msg, X), f32),
@@ -449,24 +510,23 @@
             pltpu.VMEM((3, B, F * npr, S, X), f32),
             pltpu.VMEM((B, F * npr, S, X), f32),
             pltpu.VMEM((S * ret, X), f32),
-            pltpu.VMEM((W * ret, X), f32),
+            pltpu.VMEM((W * kept, X), f32),
             pltpu.VMEM((NMOM * D * F, B, X), f32),
-            pltpu.VMEM((R, X), f32),
-            pltpu.VMEM((T, R, X), f32),
-            pltpu.VMEM((S, R, X), f32),
+            pltpu.VMEM((S * T, 1, B * R), f32),
+            dma((8,)),
             dma((S * T,)),
             dma((T, S)),
             dma((3,)),
             dma((3,)),
             dma((W,)),
             dma((W,)),
-            dma((T,)),
-            dma((T,)),
             dma((S,)),
             dma((S,)),
+            dma((S * T,)),
+            dma((S * T,)),
         ],
         compiler_params=pltpu.CompilerParams(
-            collective_id=0, has_side_effects=True, vmem_limit_bytes=48 * 1024 * 1024
+            collective_id=0, has_side_effects=True, vmem_limit_bytes=63 * 1024 * 1024
         ),
     )(
         strain_ids,
@@ -476,12 +536,12 @@
         probes.reshape(B * R, X),
         test_block.reshape(B * R, X),
         band_edge.reshape(B, X),
-        strain_elastic[0],
+        jnp.transpose(strain_elastic[0], (1, 0, 2)),
     )
     fields = fields.reshape(NFIELD, 1, 1, B, R, 1, X)
     fields = jnp.concatenate([fields, jnp.zeros_like(fields)], axis=1)
-    proj = proj[:, : NMOM * R].reshape(R, W, NMOM, npr)
-    proj = jnp.transpose(proj, (2, 0, 1, 3)).reshape(NMOM, 1, R, R)
+    proj = proj[:, : NMOM * npr * R].reshape(W, NMOM, npr, R)
+    proj = jnp.transpose(proj, (1, 3, 0, 2)).reshape(NMOM, 1, R, R)
     return fields, jnp.concatenate([proj, jnp.zeros_like(proj)], axis=1)
 
 

time: 38.4 us -> 34.4 us (0.90)
  local copies, waits for them, and re-layouts: 5.41 us -> 2.59 us
  Pallas kernels: 32 us -> 31 us
    unnamed x16 -> x3, local copies, waits for them, and re-layouts: 3.82 us -> 0.08 us
    pallas_call x1, Pallas kernels: 32 us -> 31 us  [on_device(): pl.pallas_call(functools.partial(kernel, dims), out_shape=(jax.ShapeDtype...]
    concatenate x1, local copies, waits for them, and re-layouts: 0.85 us -> 1.76 us  [on_device(): fields = jnp.concatenate([fields, jnp.zeros_like(fields)], axis=1)]
where the time goes in v2:
time: 34.4 us; the launch traced here: 34.2 us
  Pallas kernels  31 us (90%)
  local copies, waits for them, and re-layouts  2.59 us (8%)
  between operations  0.66 us (2%)
    pallas_call x1, Pallas kernels, on_device(): pl.pallas_call(functools.partial(kernel, dims), out_shape=(jax.ShapeDtype...  31 us
    concatenate x1, local copies, waits for them, and re-layouts, on_device(): fields = jnp.concatenate([fields, jnp.zeros_like(fields)], axis=1)  1.76 us

profile of v2, /device:TPU:0, one launch (start us, length us, event | category | flops | bytes accessed | tf_op | source)
XLA Modules:
  0.0 34.2 jit_solution(18254769162678334613)
XLA Ops:
  0.6 31.0 %shard_map.95 = (f32[256,128]{1,0:T(8,128)}, f32[8,128]{1,0:T(8,128)}) custom-call(s32[16]{0:T(128)} %ids_in.1, f32[8]{0:T(128)} %hop_in.1, f32[2,8,8]{2,1,0:T(8,128)} %cross_in.1, f32[6,8,8]{2,1,0:T(8,128)} %deform_in.1, f32[128,128]{1,0:T(8,128)} %bitcast.14, f32[128,128]{1,0:T(8,128)} %bitcast.15, f32[8,128]{1,0:T(8,128)} %bitcast.17, f32[6,4,32]{2,1,0:T(4,128)} %bitcast.16), custom_call_target="tpu_custom_call" | custom-call | tf_op jit(solution)/shard_map/pallas_call | solution.py:488
  31.6 0.0 copy-start
  31.6 1.8 %concatenate.6 = f32[2,2,1,8,16,1,128]{6,5,4,3,2,1,0:T(1,128)} pad(f32[2,1,1,8,16,1,128]{6,5,4,3,2,1,0:T(1,128)} %bitcast.12, f32[]{:T(128)} %constant.1.clone.1), padding=0_0x0_1x0_0x0_0x0_0x0_0x0_0 | pad | bytes 393220 | tf_op jit(solution)/shard_map/concatenate | solution.py:542
  33.4 0.0 copy-done
  33.4 0.1 reshape.26
  33.5 0.1 copy.15
  33.6 0.6 %concatenate.7.clone = f32[4,2,16,16]{3,2,1,0:T(8,128)} pad(f32[4,1,16,16]{3,2,1,0:T(8,128)S(1)} %copy.15, f32[]{:T(128)} %constant.1.clone.1), padding=0_0x0_1x0_0x0_0 | pad | bytes 12292 | tf_op jit(solution)/shard_map/concatenate | solution.py:545
  (1 shorter events, 0.0 us)
Async XLA Ops:
  31.6 1.8 %copy-start = (f32[8,128]{1,0:T(8,128)S(1)}, f32[8,128]{1,0:T(8,128)}, u32[]{:S(2)}) copy-start(f32[8,128]{1,0:T(8,128)} %get-tuple-element.5) | copy-start | bytes 12292

commit v3 on v2

--- a/solution.py
+++ b/solution.py
@@ -119,14 +119,18 @@
         load.start()
     barrier = pltpu.get_barrier_semaphore()
 
-    def greet(off, carry):
-        other = lax.rem(me + off, N)
-        pl.semaphore_signal(
-            barrier, inc=1, device_id=(other // T, lax.rem(other, T)), device_id_type=MESH
-        )
-        return carry
-
-    lax.fori_loop(1, N, greet, 0)
+    def others(act):
+        for there_tile in range(T):
+
+            def body(off, carry, there_tile=there_tile):
+                act(there_tile, lax.rem(cut + off, S))
+                return carry
+
+            lax.fori_loop(jnp.where(tile == there_tile, 1, 0), S, body, 0)
+
+    others(
+        lambda t, c: pl.semaphore_signal(barrier, inc=1, device_id=(c, t), device_id_type=MESH)
+    )
 
     slots[...] = jnp.zeros_like(slots)
     for load in loads[:3]:
@@ -157,15 +161,15 @@
 
     pl.semaphore_wait(barrier, N - 1)
 
-    def message(target_tile, target_cut, off, near):
+    def message(target_tile, target_cut, near):
         source = (target_tile * W + lax.rem(target_cut, W)) * msg
         landing = (tile * S + cut) * msg
         skip = 0 if near else chunk
         return pltpu.make_async_remote_copy(
             src_ref=send.at[pl.ds(pl.multiple_of(source + skip, 8), msg - skip), :],
             dst_ref=got.at[pl.ds(pl.multiple_of(landing + skip, 8), msg - skip), :],
-            send_sem=send_sem.at[off],
-            recv_sem=got_sem.at[tile, cut],
+            send_sem=send_sem.at[0],
+            recv_sem=got_sem.at[tile],
             device_id=(target_cut, target_tile),
             device_id_type=MESH,
         )
@@ -184,25 +188,45 @@
     for side in (0, 2):
         pl.when(has_side[side])(lambda side=side: edge_copy(side).start())
 
-    def each_other(act):
-        def body(off, carry):
-            other = lax.rem(me + off, N)
-            there_cut, there_tile = other // T, lax.rem(other, T)
-            near = jnp.abs(there_tile - tile) <= 1
-
-            @pl.when(near)
-            def _():
-                act(there_tile, there_cut, off, True)
-
-            @pl.when(jnp.logical_not(near))
-            def _():
-                act(there_tile, there_cut, off, False)
-
-            return carry
-
-        lax.fori_loop(1, N, body, 0)
-
-    each_other(lambda t, c, off, near: message(t, c, off, near).start())
+    for there in range(T):
+        near = jnp.abs(tile - there) <= 1
+        low = jnp.where(tile == there, 1, 0)
+
+        def pushes(near, there=there, low=low):
+            def body(off, carry):
+                message(there, lax.rem(cut + off, S), near).start()
+                return carry
+
+            lax.fori_loop(low, S, body, 0)
+
+        pl.when(near)(lambda pushes=pushes: pushes(True))
+        pl.when(jnp.logical_not(near))(lambda pushes=pushes: pushes(False))
+
+    def awaited(ref, send, recv):
+        return pltpu.make_async_remote_copy(
+            src_ref=ref,
+            dst_ref=ref,
+            send_sem=send,
+            recv_sem=recv,
+            device_id=(cut, tile),
+            device_id_type=MESH,
+        )
+
+    def settle(act):
+        for there in range(T):
+            gap = jnp.abs(tile - there)
+            for wanted, rows in (
+                (gap == 0, (S - 1) * msg),
+                (gap == 1, S * msg),
+                (gap > 1, S * (msg - chunk)),
+            ):
+                place = got.at[pl.ds(there * S * msg, rows), :]
+                pl.when(wanted)(
+                    lambda place=place, there=there: act(
+                        awaited(place, send_sem.at[0], got_sem.at[there])
+                    )
+                )
+
     here = pl.multiple_of((tile * S + cut) * msg, 8)
     mine = pl.multiple_of((tile * W + lax.rem(cut, W)) * msg, 8)
     got[pl.ds(here, msg), :] = send[pl.ds(mine, msg), :]
@@ -235,19 +259,7 @@
             edge_copy(2 - side).wait_recv()
             fill_green(side)
 
-    def arrived(t, c, off, near):
-        skip = 0 if near else chunk
-        place = got.at[pl.ds(pl.multiple_of((t * S + c) * msg + skip, 8), msg - skip), :]
-        pltpu.make_async_remote_copy(
-            src_ref=place,
-            dst_ref=place,
-            send_sem=send_sem.at[off],
-            recv_sem=got_sem.at[t, c],
-            device_id=(c, t),
-            device_id_type=MESH,
-        ).wait_recv()
-
-    each_other(arrived)
+    settle(lambda copy: copy.wait_recv())
 
     def run(low, high, act):
         def body(off, carry):
@@ -256,19 +268,18 @@
 
         lax.fori_loop(low, high, body, 0)
 
-    def test_copy(off, inbound):
+    def test_copy(off):
         other = lax.rem(cut + off, S)
-        landing = pl.multiple_of((other if inbound else cut) * (B * R), 8)
         return pltpu.make_async_remote_copy(
             src_ref=tests.at[own_tests, :],
-            dst_ref=tests.at[pl.ds(landing, B * R), :],
-            send_sem=test_send.at[off],
-            recv_sem=test_sem.at[other if inbound else cut],
+            dst_ref=tests.at[own_tests, :],
+            send_sem=test_send.at[0],
+            recv_sem=test_sem.at[0],
             device_id=(other, tile),
             device_id_type=MESH,
         )
 
-    run(1, S, lambda off: test_copy(off, False).start())
+    run(1, S, lambda off: test_copy(off).start())
 
     def solve_row(row):
         base = (tile + row - 1) * (S * msg)
@@ -385,25 +396,27 @@
     mates = (cut // W) * W
     rank = lax.rem(cut, W)
 
-    def home_copy(off, inbound):
+    landing = pl.multiple_of(rank * kept, 8)
+
+    def home_copy(off):
         other = lax.rem(rank + off, W)
         source = pl.multiple_of((mates + other) * ret, 8)
-        landing = pl.multiple_of((other if inbound else rank) * kept, 8)
         return pltpu.make_async_remote_copy(
             src_ref=back.at[pl.ds(source, kept), :],
             dst_ref=home.at[pl.ds(landing, kept), :],
-            send_sem=back_send.at[off],
-            recv_sem=home_sem.at[other if inbound else rank],
+            send_sem=back_send.at[0],
+            recv_sem=home_sem.at[0],
             device_id=(mates + other, tile),
             device_id_type=MESH,
         )
 
-    run(1, W, lambda off: home_copy(off, False).start())
-    home[pl.ds(pl.multiple_of(rank * kept, 8), kept), :] = back[
+    run(1, W, lambda off: home_copy(off).start())
+    home[pl.ds(landing, kept), :] = back[
         pl.ds(pl.multiple_of(cut * ret, 8), kept), :
     ]
 
-    run(1, S, lambda off: test_copy(off, True).wait_recv())
+    all_tests = awaited(tests.at[pl.ds(0, (S - 1) * B * R), :], test_send.at[0], test_sem.at[0])
+    all_tests.wait_recv()
 
     def halves(values):
         high = values.astype(jnp.bfloat16)
@@ -414,13 +427,14 @@
             left, right, (((1,), (1,)), ((), ())), preferred_element_type=jnp.float32
         )
 
-    def project(s, acc):
-        high, low = halves(back[pl.ds(pl.multiple_of(s * ret, 8), ret), :])
-        test_high, test_low = halves(tests[pl.ds(pl.multiple_of(s * (B * R), 8), B * R), :])
-        small = product(high, test_low) + product(low, test_high)
-        return acc + (small + product(high, test_high))
-
-    acc = lax.fori_loop(0, S, project, jnp.zeros((ret, B * R), jnp.float32))
+    def by_slice(ref, rows):
+        return halves(
+            jnp.concatenate([ref[s * rows : (s + 1) * rows, :] for s in range(S)], axis=1)
+        )
+
+    high, low = by_slice(back, ret)
+    test_high, test_low = by_slice(tests, B * R)
+    acc = product(high, test_low) + product(low, test_high) + product(high, test_high)
     acc = acc.reshape(NMOM * npr, B, B * R)
     lane_band = lax.broadcasted_iota(jnp.int32, acc.shape, 2) // R
     same = lane_band == lax.broadcasted_iota(jnp.int32, acc.shape, 1)
@@ -433,38 +447,39 @@
     total = jnp.sum(jnp.where(chosen, total, 0.0), axis=0, keepdims=True)
     parts_all[me] = total * ((S * B * T * X) ** (-0.5))
 
-    def part_copy(off, inbound):
-        other = lax.rem(me + off, N)
+    def part_copy(there_tile, there_cut):
         return pltpu.make_async_remote_copy(
             src_ref=parts_all.at[me],
-            dst_ref=parts_all.at[other if inbound else me],
-            send_sem=part_send.at[off],
-            recv_sem=part_sem.at[other if inbound else me],
-            device_id=(other // T, lax.rem(other, T)),
+            dst_ref=parts_all.at[me],
+            send_sem=part_send.at[0],
+            recv_sem=part_sem.at[0],
+            device_id=(there_cut, there_tile),
             device_id_type=MESH,
         )
 
-    run(1, N, lambda off: part_copy(off, False).start())
-
-    run(1, W, lambda off: home_copy(off, True).wait_recv())
+    others(lambda t, c: part_copy(t, c).start())
+
+    all_home = awaited(home.at[pl.ds(0, (W - 1) * kept), :], back_send.at[0], home_sem.at[0])
+    all_home.wait_recv()
     for w in range(W):
         for p in range(NFIELD):
             for i in range(npr):
                 row = w * kept + (p * npr + i) * B
                 field_ref[pl.ds(p * B * R + w * npr + i, B, stride=R), :] = home[row : row + B, :]
 
-    each_other(lambda t, c, off, near: message(t, c, off, near).wait_send())
+    settle(lambda copy: copy.wait_send())
     for side in (0, 2):
         pl.when(has_side[side])(lambda side=side: edge_copy(side).wait_send())
-    run(1, S, lambda off: test_copy(off, False).wait_send())
-    run(1, W, lambda off: home_copy(off, False).wait_send())
-    run(1, N, lambda off: part_copy(off, True).wait_recv())
+    all_tests.wait_send()
+    all_home.wait_send()
+    all_parts = awaited(parts_all.at[pl.ds(0, N - 1)], part_send.at[0], part_sem.at[0])
+    all_parts.wait_recv()
     for w in range(W):
         total = parts_all[w * T]
         for t in range(1, T):
             total = total + parts_all[w * T + t]
         proj_ref[w : w + 1, :] = total
-    run(1, N, lambda off: part_copy(off, False).wait_send())
+    all_parts.wait_send()
 
 
 def on_device(
@@ -514,16 +529,16 @@
             pltpu.VMEM((NMOM * D * F, B, X), f32),
             pltpu.VMEM((S * T, 1, B * R), f32),
             dma((8,)),
-            dma((S * T,)),
-            dma((T, S)),
+            dma((1,)),
+            dma((T,)),
             dma((3,)),
             dma((3,)),
-            dma((W,)),
-            dma((W,)),
-            dma((S,)),
-            dma((S,)),
-            dma((S * T,)),
-            dma((S * T,)),
+            dma((1,)),
+            dma((1,)),
+            dma((1,)),
+            dma((1,)),
+            dma((1,)),
+            dma((1,)),
         ],
         compiler_params=pltpu.CompilerParams(
             collective_id=0, has_side_effects=True, vmem_limit_bytes=63 * 1024 * 1024

time: 34.4 us -> 30.7 us (0.89)
  Pallas kernels: 31 us -> 27.2 us
    pallas_call x1, Pallas kernels: 31 us -> 27.2 us  [on_device(): pl.pallas_call(functools.partial(kernel, dims), out_shape=(jax.ShapeDtype...]
where the time goes in v3:
time: 30.7 us; the launch traced here: 30.5 us
  Pallas kernels  27.2 us (89%)
  local copies, waits for them, and re-layouts  2.59 us (8%)
  between operations  0.66 us (2%)
    pallas_call x1, Pallas kernels, on_device(): pl.pallas_call(functools.partial(kernel, dims), out_shape=(jax.ShapeDtype...  27.2 us
    concatenate x1, local copies, waits for them, and re-layouts, on_device(): fields = jnp.concatenate([fields, jnp.zeros_like(fields)], axis=1)  1.76 us
    concatenate x1, local copies, waits for them, and re-layouts, on_device(): return (fields, jnp.concatenate([proj, jnp.zeros_like(proj)], axis=1))  0.64 us

profile of v3, /device:TPU:0, one launch (start us, length us, event | category | flops | bytes accessed | tf_op | source)
XLA Modules:
  0.0 30.5 jit_solution(7197423874000696495)
XLA Ops:
  0.6 27.2 %shard_map.95 = (f32[256,128]{1,0:T(8,128)}, f32[8,128]{1,0:T(8,128)}) custom-call(s32[16]{0:T(128)} %ids_in.1, f32[8]{0:T(128)} %hop_in.1, f32[2,8,8]{2,1,0:T(8,128)} %cross_in.1, f32[6,8,8]{2,1,0:T(8,128)} %deform_in.1, f32[128,128]{1,0:T(8,128)} %bitcast.14, f32[128,128]{1,0:T(8,128)} %bitcast.15, f32[8,128]{1,0:T(8,128)} %bitcast.17, f32[6,4,32]{2,1,0:T(4,128)} %bitcast.16), custom_call_target="tpu_custom_call" | custom-call | tf_op jit(solution)/shard_map/pallas_call | solution.py:503
  27.9 0.0 copy-start
  27.9 1.8 %concatenate.6 = f32[2,2,1,8,16,1,128]{6,5,4,3,2,1,0:T(1,128)} pad(f32[2,1,1,8,16,1,128]{6,5,4,3,2,1,0:T(1,128)} %bitcast.12, f32[]{:T(128)} %constant.1.clone.1), padding=0_0x0_1x0_0x0_0x0_0x0_0x0_0 | pad | bytes 393220 | tf_op jit(solution)/shard_map/concatenate | solution.py:557
  29.6 0.0 copy-done
  29.6 0.1 reshape.26
  29.8 0.1 copy.15
  29.8 0.6 %concatenate.7.clone = f32[4,2,16,16]{3,2,1,0:T(8,128)} pad(f32[4,1,16,16]{3,2,1,0:T(8,128)S(1)} %copy.15, f32[]{:T(128)} %constant.1.clone.1), padding=0_0x0_1x0_0x0_0 | pad | bytes 12292 | tf_op jit(solution)/shard_map/concatenate | solution.py:560
  (1 shorter events, 0.0 us)
Async XLA Ops:
  27.9 1.8 %copy-start = (f32[8,128]{1,0:T(8,128)S(1)}, f32[8,128]{1,0:T(8,128)}, u32[]{:S(2)}) copy-start(f32[8,128]{1,0:T(8,128)} %get-tuple-element.5) | copy-start | bytes 12292

commit v4 on v3

--- a/solution.py
+++ b/solution.py
@@ -240,7 +240,7 @@
         parts = line_green(edges[row], hop, S)
         for f in range(F):
             for d in range(D):
-                green[row, f * D + d] = parts[f][d]
+                green[row, pl.ds(d * F + f, B, stride=D * F), :] = parts[f][d]
         return parts
 
     parts = fill_green(1)
@@ -250,8 +250,10 @@
             wi = 2.0 * math.sin((p + 1) * ANGLES[j]) / PTS
             for d in range(D):
                 re, im = parts[2 * j][d], parts[2 * j + 1][d]
-                final[(p * D + d) * F + 2 * j] = wr * re - wi * im
-                final[(p * D + d) * F + 2 * j + 1] = -(wr * im + wi * re)
+                final[pl.ds((p * D + d) * F + 2 * j, B, stride=NMOM * D * F), :] = wr * re - wi * im
+                final[pl.ds((p * D + d) * F + 2 * j + 1, B, stride=NMOM * D * F), :] = -(
+                    wr * im + wi * re
+                )
     for side in (0, 2):
 
         @pl.when(has_side[side])
@@ -293,10 +295,13 @@
                     pairs.append(pltpu.roll(line, d, 0) + pltpu.roll(line, S - d, 0))
                 pairs.append(pltpu.roll(line, half, 0))
                 sums.append(pairs)
+            factors = [
+                green[row, pl.ds(pl.multiple_of((b * D + d) * F, 8), F), :] for d in range(D)
+            ]
             for f in range(F):
                 totals = [None] * npr
                 for d in range(D):
-                    factor = green[row, f * D + d, pl.ds(b, 1), :]
+                    factor = factors[d][f : f + 1]
                     for i in range(npr):
                         term = factor * sums[i][d]
                         totals[i] = term if totals[i] is None else totals[i] + term
@@ -374,8 +379,10 @@
                     totals[i] = term if totals[i] is None else totals[i] + term
             for d in range(D):
                 zs = [None] * npr
+                start = pl.multiple_of(((b * NMOM + p) * D + d) * F, 8)
+                factors = final[pl.ds(start, F), :]
                 for f in range(F):
-                    factor = final[(p * D + d) * F + f, pl.ds(b, 1), :]
+                    factor = factors[f : f + 1]
                     for i in range(npr):
                         term = factor * ys[i][f]
                         zs[i] = term if zs[i] is None else zs[i] + term
@@ -480,6 +487,41 @@
             total = total + parts_all[w * T + t]
         proj_ref[w : w + 1, :] = total
     all_parts.wait_send()
+
+
+def emit(npr, field_in, proj_in, field_out, proj_out, zeros, held, sems):
+    W, columns = held.shape
+    R = proj_out.shape[-1]
+    load = pltpu.make_async_copy(proj_in, held, sems.at[0])
+    load.start()
+    copies = []
+    for p in range(NFIELD):
+        copies.append(
+            pltpu.make_async_copy(field_in.at[p], field_out.at[p, 0], sems.at[1 + 2 * p])
+        )
+        copies[-1].start()
+    zeros[...] = jnp.zeros_like(zeros)
+    for p in range(NFIELD):
+        copies.append(pltpu.make_async_copy(zeros, field_out.at[p, 1], sems.at[2 + 2 * p]))
+        copies[-1].start()
+    load.wait()
+    turned = jnp.transpose(held[...])
+    worker = lax.broadcasted_iota(jnp.int32, (W, R), 0) * npr
+    column = lax.broadcasted_iota(jnp.int32, (W, R), 1)
+    spread = []
+    for i in range(npr):
+        placing = jnp.where(column == worker + i, 1.0, 0.0)
+        spread.append(jnp.dot(turned, placing, precision=lax.Precision.HIGHEST))
+    for p in range(NMOM):
+        total = None
+        for i in range(npr):
+            row = (p * npr + i) * R
+            term = spread[i][row : row + R]
+            total = term if total is None else total + term
+        proj_out[p, 0] = total
+        proj_out[p, 1] = jnp.zeros_like(total)
+    for copy in copies:
+        copy.wait()
 
 
 def on_device(
@@ -520,13 +562,13 @@
             pltpu.VMEM((T * W * msg, X), f32),
             pltpu.VMEM((T * S * msg, X), f32),
             pltpu.VMEM((3, B, X), f32),
-            pltpu.VMEM((3, F * D, B, X), f32),
+            pltpu.VMEM((3, B * D * F, X), f32),
             pltpu.VMEM((B, B, S, X), f32),
             pltpu.VMEM((3, B, F * npr, S, X), f32),
             pltpu.VMEM((B, F * npr, S, X), f32),
             pltpu.VMEM((S * ret, X), f32),
             pltpu.VMEM((W * kept, X), f32),
-            pltpu.VMEM((NMOM * D * F, B, X), f32),
+            pltpu.VMEM((B * NMOM * D * F, X), f32),
             pltpu.VMEM((S * T, 1, B * R), f32),
             dma((8,)),
             dma((1,)),
@@ -553,11 +595,22 @@
         band_edge.reshape(B, X),
         jnp.transpose(strain_elastic[0], (1, 0, 2)),
     )
-    fields = fields.reshape(NFIELD, 1, 1, B, R, 1, X)
-    fields = jnp.concatenate([fields, jnp.zeros_like(fields)], axis=1)
-    proj = proj[:, : NMOM * npr * R].reshape(W, NMOM, npr, R)
-    proj = jnp.transpose(proj, (1, 3, 0, 2)).reshape(NMOM, 1, R, R)
-    return fields, jnp.concatenate([proj, jnp.zeros_like(proj)], axis=1)
+    fields, proj = pl.pallas_call(
+        functools.partial(emit, npr),
+        out_shape=(
+            jax.ShapeDtypeStruct((NFIELD, 2, B * R, X), f32),
+            jax.ShapeDtypeStruct((NMOM, 2, R, R), f32),
+        ),
+        in_specs=[hbm] * 2,
+        out_specs=(hbm, vmem),
+        scratch_shapes=[
+            pltpu.VMEM((B * R, X), f32),
+            pltpu.VMEM((W, B * R), f32),
+            dma((1 + 2 * NFIELD,)),
+        ],
+        compiler_params=pltpu.CompilerParams(vmem_limit_bytes=63 * 1024 * 1024),
+    )(fields.reshape(NFIELD, B * R, X), proj)
+    return fields.reshape(NFIELD, 2, 1, B, R, 1, X), proj
 
 
 def solution(mesh):

time: 30.7 us -> 33.9 us (1.10)
  Pallas kernels: 27.2 us -> 33 us
  local copies, waits for them, and re-layouts: 2.59 us -> 0 us
    pallas_call x0 -> x1, Pallas kernels: none -> 5.75 us  [on_device(): pl.pallas_call(functools.partial(emit, npr), out_shape=(jax.ShapeDtypeStr...]
    concatenate x2 -> x0, local copies, waits for them, and re-layouts: 2.4 us -> none  [the longest x1 1.76 us: on_device(): fields = jnp.concatenate([fields, jnp.zeros_like(fields)], axis=1)]
where the time goes in v4:
time: 33.9 us; the launch traced here: 33.6 us
  Pallas kernels  33 us (97%)
  between operations  0.64 us (2%)
    pallas_call x1, Pallas kernels, on_device(): pl.pallas_call(functools.partial(kernel, dims), out_shape=(jax.ShapeDtype...  27.2 us
    pallas_call x1, Pallas kernels, on_device(): pl.pallas_call(functools.partial(emit, npr), out_shape=(jax.ShapeDtypeStr...  5.75 us

profile of v4, /device:TPU:0, one launch (start us, length us, event | category | flops | bytes accessed | tf_op | source)
XLA Modules:
  0.0 33.6 jit_solution(13377798861428665395)
XLA Ops:
  0.6 27.2 %shard_map.95 = (f32[256,128]{1,0:T(8,128)}, f32[8,128]{1,0:T(8,128)}) custom-call(s32[16]{0:T(128)} %ids_in.1, f32[8]{0:T(128)} %hop_in.1, f32[2,8,8]{2,1,0:T(8,128)} %cross_in.1, f32[6,8,8]{2,1,0:T(8,128)} %deform_in.1, f32[128,128]{1,0:T(8,128)} %bitcast.11, f32[128,128]{1,0:T(8,128)} %bitcast.12, f32[8,128]{1,0:T(8,128)} %bitcast.14, f32[6,4,32]{2,1,0:T(4,128)} %bitcast.13), custom_call_target="tpu_custom_call" | custom-call | tf_op jit(solution)/shard_map/pallas_call | solution.py:545
  27.9 5.7 %shard_map.96 = (f32[2,2,128,128]{3,2,1,0:T(8,128)}, f32[4,2,16,16]{3,2,1,0:T(8,128)}) custom-call(f32[2,128,128]{2,1,0:T(8,128)} %bitcast.10, f32[8,128]{1,0:T(8,128)} %get-tuple-element.7.proj_in), custom_call_target="tpu_custom_call" | custom-call | tf_op jit(solution)/shard_map/pallas_call | solution.py:598

commit v5 on v3

--- a/solution.py
+++ b/solution.py
@@ -252,15 +252,6 @@
                 re, im = parts[2 * j][d], parts[2 * j + 1][d]
                 final[(p * D + d) * F + 2 * j] = wr * re - wi * im
                 final[(p * D + d) * F + 2 * j + 1] = -(wr * im + wi * re)
-    for side in (0, 2):
-
-        @pl.when(has_side[side])
-        def _(side=side):
-            edge_copy(2 - side).wait_recv()
-            fill_green(side)
-
-    settle(lambda copy: copy.wait_recv())
-
     def run(low, high, act):
         def body(off, carry):
             act(off)
@@ -280,6 +271,15 @@
         )
 
     run(1, S, lambda off: test_copy(off).start())
+
+    for side in (0, 2):
+
+        @pl.when(has_side[side])
+        def _(side=side):
+            edge_copy(2 - side).wait_recv()
+            fill_green(side)
+
+    settle(lambda copy: copy.wait_recv())
 
     def solve_row(row):
         base = (tile + row - 1) * (S * msg)

time: 30.7 us -> 27.3 us (0.89)
  Pallas kernels: 27.2 us -> 23.9 us
    pallas_call x1, Pallas kernels: 27.2 us -> 23.9 us  [on_device(): pl.pallas_call(functools.partial(kernel, dims), out_shape=(jax.ShapeDtype...]
where the time goes in v5:
time: 27.3 us; the launch traced here: 27.1 us
  Pallas kernels  23.9 us (88%)
  local copies, waits for them, and re-layouts  2.59 us (9%)
  between operations  0.66 us (2%)
    pallas_call x1, Pallas kernels, on_device(): pl.pallas_call(functools.partial(kernel, dims), out_shape=(jax.ShapeDtype...  23.9 us
    concatenate x1, local copies, waits for them, and re-layouts, on_device(): fields = jnp.concatenate([fields, jnp.zeros_like(fields)], axis=1)  1.76 us
    concatenate x1, local copies, waits for them, and re-layouts, on_device(): return (fields, jnp.concatenate([proj, jnp.zeros_like(proj)], axis=1))  0.64 us

profile of v5, /device:TPU:0, one launch (start us, length us, event | category | flops | bytes accessed | tf_op | source)
XLA Modules:
  0.0 27.1 jit_solution(5312541346134661598)
XLA Ops:
  0.6 23.9 %shard_map.95 = (f32[256,128]{1,0:T(8,128)}, f32[8,128]{1,0:T(8,128)}) custom-call(s32[16]{0:T(128)} %ids_in.1, f32[8]{0:T(128)} %hop_in.1, f32[2,8,8]{2,1,0:T(8,128)} %cross_in.1, f32[6,8,8]{2,1,0:T(8,128)} %deform_in.1, f32[128,128]{1,0:T(8,128)} %bitcast.14, f32[128,128]{1,0:T(8,128)} %bitcast.15, f32[8,128]{1,0:T(8,128)} %bitcast.17, f32[6,4,32]{2,1,0:T(4,128)} %bitcast.16), custom_call_target="tpu_custom_call" | custom-call | tf_op jit(solution)/shard_map/pallas_call | solution.py:503
  24.5 0.0 copy-start
  24.5 1.8 %concatenate.6 = f32[2,2,1,8,16,1,128]{6,5,4,3,2,1,0:T(1,128)} pad(f32[2,1,1,8,16,1,128]{6,5,4,3,2,1,0:T(1,128)} %bitcast.12, f32[]{:T(128)} %constant.1.clone.1), padding=0_0x0_1x0_0x0_0x0_0x0_0x0_0 | pad | bytes 393220 | tf_op jit(solution)/shard_map/concatenate | solution.py:557
  26.3 0.0 copy-done
  26.3 0.1 reshape.26
  26.4 0.1 copy.15
  26.5 0.6 %concatenate.7.clone = f32[4,2,16,16]{3,2,1,0:T(8,128)} pad(f32[4,1,16,16]{3,2,1,0:T(8,128)S(1)} %copy.15, f32[]{:T(128)} %constant.1.clone.1), padding=0_0x0_1x0_0x0_0 | pad | bytes 12292 | tf_op jit(solution)/shard_map/concatenate | solution.py:560
  (1 shorter events, 0.0 us)
Async XLA Ops:
  24.5 1.8 %copy-start = (f32[8,128]{1,0:T(8,128)S(1)}, f32[8,128]{1,0:T(8,128)}, u32[]{:S(2)}) copy-start(f32[8,128]{1,0:T(8,128)} %get-tuple-element.5) | copy-start | bytes 12292
